TPU v7x, 512 devices: a whole 4x4x16 slice. The times are simulated.
512 devices in a mesh: day: 4 (over z_hi), row: 16 (over y, z_lo), col: 8 (over x, core).
Axes of the slice: x: 4, y: 4, z: 16 (z_hi: 4, z_lo: 4; z = z_hi * 4 + z_lo), core: 2. Of those that a mesh axis runs over, the one named last changes fastest.
Arguments:
- returns: float32 [8, 512, 8192], P('day', None, ('row', 'col')), may hold values from -100 to 100
- traded: int32 [8, 512, 8192], P('day', None, ('row', 'col')), may hold values 0 or 1
Outputs:
- covariance: float32 [8, 8192, 8192], P('day', 'row', 'col')
All inputs are finite; a program needn't handle non-finite values. No bound on the sum of `traded` on one device may be relied on, other than what follows from the above.
Results may differ from a plain program's by a relative error of at most 0.000086.
Values sent between devices are 32-bit elements; how exact they have to be, the bound alone decides.
No kernel may reach another device: no remote copies, remote signals or barrier semaphores. Data moves between devices by JAX's collectives and lax.ppermute only.
A program may use at most 64 MiB of HBM per device.

v0:
```python
import jax
import jax.numpy as jnp
from jax import lax
from jax.sharding import PartitionSpec as P


def broadcast(value, axis, source):
    kept = jnp.where(lax.axis_index(axis) == source, value, 0).astype(value.dtype)
    return lax.psum(kept, axis)


def tile_product(left, right):
    return jnp.einsum(
        "dbi,dbj->dij",
        left,
        right,
        preferred_element_type=jnp.float32,
        precision=lax.Precision.HIGHEST,
    )


def body(returns, traded):
    live = traded.astype(jnp.float32)
    absolute = jnp.sum(live * jnp.abs(returns), axis=0)
    count = jnp.sum(live, axis=0)
    absolute, count = lax.psum((absolute, count), "day")
    level = absolute / jnp.maximum(count, 1.0)
    profile = level / jnp.sqrt(jnp.mean(level * level, axis=0, keepdims=True) + 1e-06)
    scaled = live * returns / jnp.maximum(profile, 0.2)
    row_assets = lax.all_gather(scaled, "col", axis=2, tiled=True)
    ratio = lax.axis_size("row") // lax.axis_size("col")
    first_root = lax.axis_index("col") * ratio
    panels = []
    for offset in range(ratio):
        panels.append(broadcast(row_assets, "row", first_root + offset))
    column_assets = jnp.concatenate(panels, axis=2)
    return tile_product(row_assets, column_assets)


def solution(mesh):
    in_specs = (P("day", None, ("row", "col")), P("day", None, ("row", "col")))
    out_specs = P("day", "row", "col")
    return jax.shard_map(body, mesh=mesh, in_specs=in_specs, out_specs=out_specs, check_vma=False)
```

profile of v0, /device:TPU:1, one launch (start us, length us, event | category | flops | bytes accessed | tf_op | source)
XLA Modules:
  0.0 356.3 jit_solution(485485752401044991)
XLA Ops:
  6.5 0.0 all-reduce.7.cloned.1.call-start
  6.5 1.8 convert_reduce_fusion
  8.3 0.0 all-reduce.7.cloned.1.call-update
  8.4 0.0 all-gather.2.cloned.1.call-start
  8.4 77.0 %all-reduce.7.cloned.1.call-done = (f32[512,64]{0,1:T(8,128)}, f32[512,64]{0,1:T(8,128)}) async-done(((f32[512,64]{0,1:T(8,128)}, f32[512,64]{0,1:T(8,128)}), (f32[512,64]{0,1:T(8,128)}, f32[512,64]{0,1:T(8,128)})) %all-reduce.7.cloned.1.call-update) | async-done | bytes 262160 | tf_op jit(solution)/shard_map/psum | solution.py:26
  85.4 1.1 multiply_reduce_fusion.1
  86.6 1.1 divide_maximum_fusion
  87.6 1.1 multiply_divide_fusion
  88.7 0.9 copy.13
  89.6 0.0 all-gather.2.cloned.1.call-update
  89.7 0.0 all-reduce.5.cloned.1.call-start
  89.7 30.1 %all-gather.2.cloned.1.call-done = f32[2,512,512]{1,0,2:T(2,128)} async-done(((f32[2,512,64]{1,0,2:T(2,128)}), f32[2,512,512]{1,0,2:T(2,128)}) %all-gather.2.cloned.1.call-update) | async-done | bytes 2097168 | tf_op jit(solution)/shard_map/all_gather | solution.py:30
  119.8 2.7 copy.14
  122.6 2.7 broadcast_select_fusion.1
  125.3 0.0 all-reduce.5.cloned.1.call-update
  125.3 214.6 %all-reduce.5.cloned.1.call-done = (f32[2,512,512]{2,1,0:T(8,128)}, f32[2,512,512]{2,1,0:T(8,128)}) async-done(((f32[2,512,512]{2,1,0:T(8,128)}, f32[2,512,512]{2,1,0:T(8,128)}), (f32[2,512,512]{2,1,0:T(8,128)}, f32[2,512,512]{2,1,0:T(8,128)})) %all-reduce.5.cloned.1.call-update) | async-done | bytes 4194320 | tf_op jit(solution)/shard_map/psum | solution.py:9
  339.9 9.9 %fusion = f32[2,512,1024]{2,1,0:T(8,128)} fusion(f32[2,512,512]{2,1,0:T(8,128)S(1)} %copy.14, f32[2,512,512]{2,1,0:T(8,128)} %get-tuple-element.7, f32[2,512,512]{2,1,0:T(8,128)} %get-tuple-element.8), kind=kOutput, calls=%fused_computation | convolution fusion | flops 6443499520 | bytes 10485760 | tf_op jit(solution)/shard_map/dbi,dbj->dij/dot_general | solution.py:13
  (1 shorter events, 0.0 us)
Async XLA Ops:
  6.5 78.9 %all-reduce.7.cloned.1.call-start = ((), (), s32[]{:S(2)}) async-start(), calls=%async_computation.2 | async-start | bytes 524288 | tf_op jit(solution)/shard_map/psum | solution.py:26
  8.4 111.4 %all-gather.2.cloned.1.call-start = ((), (), s32[]{:S(2)}) async-start(), calls=%async_computation | async-start | bytes 2359296 | tf_op jit(solution)/shard_map/all_gather | solution.py:30
  89.7 250.3 %all-reduce.5.cloned.1.call-start = ((), (), s32[]{:S(2)}) async-start(), calls=%async_computation.1 | async-start | bytes 8388608 | tf_op jit(solution)/shard_map/psum | solution.py:9
Sparse Core Ops, SparseCore 0:
  10.3 75.0 all-reduce.6
  89.8 29.9 all-gather.1
  125.4 214.4 all-reduce.4
where the time goes:
time: 357 us; the launch traced here: 356 us
  waiting for transfers between devices  322 us (90%)
  between operations  13.1 us (4%)
  matrix products  9.85 us (3%)
  other arithmetic  7.8 us (2%)
  local copies, waits for them, and re-layouts  3.66 us (1%)
    psum x1, waiting for transfers between devices, broadcast(): return lax.psum(kept, axis)  215 us
    psum x1, waiting for transfers between devices, body(): absolute, count = lax.psum((absolute, count), 'day')  77 us
    all_gather x1, waiting for transfers between devices, body(): row_assets = lax.all_gather(scaled, 'col', axis=2, tiled=True)  30.1 us
    dot_general x1, matrix products, tile_product(): jnp.einsum('dbi,dbj->dij', left, right, preferred_element_type=jnp.float3...  9.85 us
  transfers between devices with their start and end apart: 3, of which 3 were waited for; matrix products, arithmetic and copies ran while one was open for 0% of the time, Pallas kernels for 0%

commit v1 on v0

v1 whole, which is shorter than its diff:
```python
import jax
import jax.numpy as jnp
from jax import lax
from jax.experimental import pallas as pl
from jax.experimental.pallas import tpu as pltpu
from jax.sharding import Mesh
from jax.sharding import PartitionSpec as P

DAY, Y, Z, X, CORE = "day", "y", "z", "x", "core"
SIZES = (4, 4, 4, 4, 2)
ALL = (DAY, Y, Z, X, CORE)
GROUP = (Y, Z, X, CORE)
N = 4
WHOLE = pl.BlockSpec(memory_space=pltpu.VMEM)
SCALARS = pl.BlockSpec(memory_space=pltpu.SMEM)


def turn_pairs():
    def place(y, z, x, core):
        return ((y * N + z) * N + x) * 2 + core

    pairs = []
    for y in range(N):
        for z in range(N):
            for x in range(N):
                for core in range(2):
                    pairs.append((place(y, z, x, core), place(x, (z % 2) * 2 + core, y, z // 2)))
    return pairs


def shift(step):
    return [(i, (i + step) % N) for i in range(N)]


def local(kernel, shapes, *blocks, after=(), specs=None):
    skip = len(after)

    def run(*refs):
        kernel(*refs[: len(blocks)], *refs[len(blocks) + skip :])

    moved = sum(4 * block.size for block in blocks) + sum(4 * shape.size for shape in shapes)
    return pl.pallas_call(
        run,
        in_specs=(specs or [WHOLE] * len(blocks)) + [pl.BlockSpec(memory_space=pl.ANY)] * skip,
        out_specs=[WHOLE] * len(shapes),
        out_shape=shapes,
        compiler_params=pltpu.CompilerParams(vmem_limit_bytes=8 * 1024 * 1024),
        cost_estimate=pl.CostEstimate(flops=moved, bytes_accessed=moved, transcendentals=0),
    )(*blocks, *after)


def sums_kernel(returns, traded, masked, sums):
    share = sums.shape[2]
    for group in range(N):
        rows = slice(group * share, (group + 1) * share)
        absolute = jnp.zeros(sums.shape[2:], jnp.float32)
        count = jnp.zeros(sums.shape[2:], jnp.float32)
        for k in range(masked.shape[0]):
            live = traded[k, rows, :].astype(jnp.float32)
            value = live * returns[k, rows, :]
            masked[k, rows, :] = value
            absolute += jnp.abs(value)
            count += live
        sums[group, 0] = absolute
        sums[group, 1] = count


def weight_kernel(sums, weight):
    absolute = (sums[0, 0] + sums[1, 0]) + (sums[2, 0] + sums[3, 0])
    count = (sums[0, 1] + sums[1, 1]) + (sums[2, 1] + sums[3, 1])
    level = absolute / jnp.maximum(count, 1.0)
    profile = level / jnp.sqrt(jnp.mean(level * level, axis=1, keepdims=True) + 1e-06)
    weight[...] = 1.0 / jnp.maximum(profile, 0.2)


def scale_kernel(masked, weight, scaled):
    for k in range(masked.shape[0]):
        scaled[k] = masked[k] * weight[...]


def pack_kernel(z1, z2, z3, y_up, y_down, up, down):
    for n, piece in enumerate((z1, z2, z3)):
        for k in range(2):
            up[2 * n + k] = piece[k]
            down[2 * n + k] = piece[k]
    up[6] = y_up[0]
    down[6] = y_down[1]


def hand_on_kernel(from_up, from_down, up, down):
    for n, (here, there) in enumerate(((0, 4), (1, 5), (2, 3))):
        up[n] = from_up[here]
        down[n] = from_down[there]


def split(value):
    high = value.astype(jnp.bfloat16)
    low = (value - high.astype(jnp.float32)).astype(jnp.bfloat16)
    return high, low


def triple(row_high, row_low, col_high, col_low):
    def dot(left, right):
        return lax.dot_general(left, right, (((1,), (1,)), ((), ())), preferred_element_type=jnp.float32)

    return dot(row_high, col_low) + dot(row_low, col_high) + dot(row_high, col_high)


def keep_columns(where, step, blocks, high, low):
    size = blocks[0].shape[0]
    for n, block in enumerate(blocks):
        part = pl.ds(pl.multiple_of(lax.rem(where[1] - n + N, N) * size, size), size)
        high[step, part, :], low[step, part, :] = split(block)


def send_columns(where, step, k, tile, out, sems):
    half = tile.shape[1] // 2
    x = lax.rem(where[0] - step + N, N)
    copies = []
    for p in range(2):
        start = pl.multiple_of((p * N + x) * half, half)
        copies.append(
            pltpu.make_async_copy(tile.at[:, p * half : (p + 1) * half], out.at[k, :, pl.ds(start, half)], sems.at[p])
        )
    return copies


def near_kernel(
    where, rows, own, z1, z2, z3, y_up, up, y_down, down, out, row_high, row_low, high, low, tiles, sems
):
    size = rows.shape[2]
    copies = []
    for k in range(2):
        for n in range(rows.shape[0]):
            part = slice(n * size, (n + 1) * size)
            row_high[k, part, :], row_low[k, part, :] = split(rows[n, k])
        groups = (
            (0, [own[k], z1[k], z2[k], z3[k]]),
            (1, [y_up[k], up[k], up[2 + k], up[4 + k]]),
            (3, [y_down[k], down[k], down[2 + k], down[4 + k]]),
        )
        for n, (step, blocks) in enumerate(groups):
            spot = 3 * k + n
            keep_columns(where, spot, blocks, high, low)
            tiles[k, n] = triple(row_high[k], row_low[k], high[spot], low[spot])
            for copy in send_columns(where, step, k, tiles.at[k, n], out, sems.at[k, n]):
                copy.start()
                copies.append(copy)
    for copy in copies:
        copy.wait()


def far_kernel(where, row_high, row_low, up, down, far_up, far_down, kept, out, high, low, tiles, sems):
    blocks = (
        [up[6], far_up[0], far_up[2], far_down[0]],
        [down[6], far_up[1], far_down[2], far_down[1]],
    )
    copies = []
    for k in range(2):
        keep_columns(where, k, blocks[k], high, low)
        tiles[k] = triple(row_high[k], row_low[k], high[k], low[k])
        for copy in send_columns(where, 2, k, tiles.at[k], out, sems.at[k]):
            copy.start()
            copies.append(copy)
    for copy in copies:
        copy.wait()


def near_product(where, rows, *blocks):
    _, days, size, bins = rows.shape
    height, width = rows.shape[0] * size, N * size
    halves = [jax.ShapeDtypeStruct((days, height, bins), jnp.bfloat16)] * 2
    return pl.pallas_call(
        near_kernel,
        in_specs=[SCALARS] + [WHOLE] * (1 + len(blocks)),
        out_specs=[pl.BlockSpec(memory_space=pl.ANY), WHOLE, WHOLE],
        out_shape=[jax.ShapeDtypeStruct((days, height, N * width), jnp.float32)] + halves,
        scratch_shapes=[
            pltpu.VMEM((3 * days, width, bins), jnp.bfloat16),
            pltpu.VMEM((3 * days, width, bins), jnp.bfloat16),
            pltpu.VMEM((days, 3, height, width), jnp.float32),
            pltpu.SemaphoreType.DMA((days, 3, 2)),
        ],
        compiler_params=pltpu.CompilerParams(vmem_limit_bytes=16 * 1024 * 1024),
        cost_estimate=pl.CostEstimate(
            flops=18 * days * height * width * bins, bytes_accessed=12 * days * height * width, transcendentals=0
        ),
    )(where, rows, *blocks)


def far_product(where, row_high, row_low, up, down, far_up, far_down, kept):
    days, height, bins = row_high.shape
    width = kept.shape[2] // N
    anywhere = pl.BlockSpec(memory_space=pl.ANY)
    return pl.pallas_call(
        far_kernel,
        in_specs=[SCALARS] + [WHOLE] * 6 + [anywhere],
        out_specs=anywhere,
        out_shape=jax.ShapeDtypeStruct(kept.shape, kept.dtype),
        input_output_aliases={7: 0},
        scratch_shapes=[
            pltpu.VMEM((days, width, bins), jnp.bfloat16),
            pltpu.VMEM((days, width, bins), jnp.bfloat16),
            pltpu.VMEM((days, height, width), jnp.float32),
            pltpu.SemaphoreType.DMA((days, 2)),
        ],
        compiler_params=pltpu.CompilerParams(vmem_limit_bytes=8 * 1024 * 1024),
        cost_estimate=pl.CostEstimate(
            flops=6 * days * height * width * bins, bytes_accessed=4 * days * height * width, transcendentals=0
        ),
    )(where, row_high, row_low, up, down, far_up, far_down, kept)


def body(returns, traded):
    returns = jnp.swapaxes(returns, 1, 2)
    traded = jnp.swapaxes(traded, 1, 2)
    days, size, bins = returns.shape
    share = size // N

    def shape(*sizes):
        return jax.ShapeDtypeStruct(sizes, jnp.float32)

    masked, sums = local(
        sums_kernel, [shape(days, size, bins), shape(N, 2, share, bins)], returns, traded, specs=[pl.BlockSpec()] * 2
    )
    sums = lax.all_to_all(sums, DAY, 0, 0)
    (weight,) = local(weight_kernel, [shape(share, bins)], sums)
    weight = lax.all_gather(weight, DAY, axis=0, tiled=True)
    (scaled,) = local(scale_kernel, [shape(days, size, bins)], masked, weight)

    rows = lax.all_gather(scaled, (X, CORE))

    turned = lax.ppermute(scaled, GROUP, turn_pairs())
    z_pieces = [lax.ppermute(turned, Z, shift(step)) for step in (1, 2, 3)]
    y_up = lax.ppermute(turned, Y, shift(1))
    y_down = lax.ppermute(turned, Y, shift(-1))
    up, down = local(pack_kernel, [shape(7, size, bins)] * 2, *z_pieces, y_up, y_down)
    up = lax.ppermute(up, Y, shift(1))
    down = lax.ppermute(down, Y, shift(-1))
    far_up, far_down = local(hand_on_kernel, [shape(3, size, bins)] * 2, up, down)
    far_up = lax.ppermute(far_up, Y, shift(1))
    far_down = lax.ppermute(far_down, Y, shift(-1))

    where = jnp.stack([lax.axis_index(Y), lax.axis_index(Z)]).astype(jnp.int32)
    out, row_high, row_low = near_product(where, rows, turned, *z_pieces, y_up, up, y_down, down)
    return far_product(where, row_high, row_low, up, down, far_up, far_down, out)


def solution(mesh):
    fine = Mesh(mesh.devices.reshape(SIZES), ALL)
    in_spec = P(DAY, None, GROUP)
    return jax.shard_map(
        body,
        mesh=fine,
        in_specs=(in_spec, in_spec),
        out_specs=P(DAY, (Y, Z), (X, CORE)),
        check_vma=False,
    )
```

time: 357 us -> 164 us (0.46)
  the two profiles are of different devices: /device:TPU:1 before, /device:TPU:68 now
where the time goes in v1:
time: 164 us; the launch traced here: 163 us
  blocking collectives  52.5 us (32%)
  waiting for transfers between devices  48.2 us (29%)
  starting transfers between devices  32.3 us (20%)
  between operations  13.6 us (8%)
  Pallas kernels  9.53 us (6%)
  local copies, waits for them, and re-layouts  7.04 us (4%)
    all_to_all x1, blocking collectives, body(): sums = lax.all_to_all(sums, DAY, 0, 0)  34.5 us
    ppermute x1, waiting for transfers between devices, body(): up = lax.ppermute(up, Y, shift(1))  18.3 us
    all_gather x1, blocking collectives, body(): weight = lax.all_gather(weight, DAY, axis=0, tiled=True)  18 us
    ppermute x1, waiting for transfers between devices, body(): turned = lax.ppermute(scaled, GROUP, turn_pairs())  14.7 us
    ppermute x3, waiting for transfers between devices, body(): z_pieces = [lax.ppermute(turned, Z, shift(step)) for step in (1, 2, 3)]  14 us
    ppermute x3, starting transfers between devices, body(): z_pieces = [lax.ppermute(turned, Z, shift(step)) for step in (1, 2, 3)]  9.98 us
    unnamed x18, local copies, waits for them, and re-layouts  7.04 us
    pallas_call x1, Pallas kernels, near_product(): pl.pallas_call(near_kernel, in_specs=[SCALARS] + [WHOLE] * (1 + len(block...  4.89 us
  transfers between devices with their start and end apart: 11, of which 6 were waited for; matrix products, arithmetic and copies ran while one was open for 0% of the time, Pallas kernels for 4%

profile of v1, /device:TPU:68, one launch (start us, length us, event | category | flops | bytes accessed | tf_op | source)
XLA Modules:
  0.0 163.2 jit_solution(16768744761922024955)
XLA Ops:
  6.5 0.9 copy-done.4
  7.5 0.9 copy-done.5
  8.5 34.5 %all_to_all.5.refs_0_ = f32[4,2,16,512]{3,2,1,0:T(8,128)S(1)} all-to-all(f32[4,2,16,512]{3,2,1,0:T(8,128)S(1)} %get-tuple-element.15), channel_id=1, replica_groups=mesh['day'=4,'y'=4,'z'=4,'x'=4,'core'=2] {'day'}, dimensions={0} | all-to-all | bytes 524288 | tf_op jit(solution)/shard_map/all_to_all | solution.py:226
  42.9 0.1 shard_map.29
  43.1 18.0 %all_gather.9.refs_1_ = f32[64,512]{1,0:T(8,128)S(1)} all-gather(f32[16,512]{1,0:T(8,128)S(1)} %shard_map.29), channel_id=1, replica_groups=mesh['day'=4,'y'=4,'z'=4,'x'=4,'core'=2] {'day'}, dimensions={0}, use_global_device_ids=true | all-gather | bytes 163840 | tf_op jit(solution)/shard_map/all_gather | solution.py:228
  61.1 0.7 shard_map.30
  61.8 1.9 %collective-permute-start = (f32[2,64,512]{2,1,0:T(8,128)}, f32[2,64,512]{2,1,0:T(8,128)S(1)}, u32[]{:S(2)}, u32[]{:S(2)}) collective-permute-start(f32[2,64,512]{2,1,0:T(8,128)} %shard_map.30), channel_id=1, source_target_pairs={{0,0},{1,8},{2,32},{3,40},{4,64},{5,72},{6,96},{7,104},{8,16},{9,2... | collective-permute-start | bytes 786440 | tf_op jit(solution)/shard_map/ppermute | solution.py:233
  63.8 14.7 %collective-permute-done.own = f32[2,64,512]{2,1,0:T(8,128)S(1)} collective-permute-done((f32[2,64,512]{2,1,0:T(8,128)}, f32[2,64,512]{2,1,0:T(8,128)S(1)}, u32[]{:S(2)}, u32[]{:S(2)}) %collective-permute-start) | collective-permute-done | bytes 262176 | tf_op jit(solution)/shard_map/ppermute | solution.py:233
  78.4 1.9 %collective-permute-start.5 = (f32[2,64,512]{2,1,0:T(8,128)S(1)}, f32[2,64,512]{2,1,0:T(8,128)S(1)}, u32[]{:S(2)}, u32[]{:S(2)}) collective-permute-start(f32[2,64,512]{2,1,0:T(8,128)S(1)} %collective-permute-done.own), channel_id=1, source_target_pairs={{0,96},{32,0},{64,32},{96,64},{1,97},{33,1},{65,33},{97,65},{2,98}... | collective-permute-start | bytes 786440 | tf_op jit(solution)/shard_map/ppermute | solution.py:236
  80.4 3.9 %collective-permute-start.4 = (f32[2,64,512]{2,1,0:T(8,128)S(1)}, f32[2,64,512]{2,1,0:T(8,128)S(1)}, u32[]{:S(2)}, u32[]{:S(2)}) collective-permute-start(f32[2,64,512]{2,1,0:T(8,128)S(1)} %collective-permute-done.own), channel_id=1, source_target_pairs={{0,32},{32,64},{64,96},{96,0},{1,33},{33,65},{65,97},{97,1},{2,34}... | collective-permute-start | bytes 786440 | tf_op jit(solution)/shard_map/ppermute | solution.py:235
  84.3 1.9 %collective-permute-start.3 = (f32[2,64,512]{2,1,0:T(8,128)S(1)}, f32[2,64,512]{2,1,0:T(8,128)S(1)}, u32[]{:S(2)}, u32[]{:S(2)}) collective-permute-start(f32[2,64,512]{2,1,0:T(8,128)S(1)} %collective-permute-done.own), channel_id=1, source_target_pairs={{0,24},{8,0},{16,8},{24,16},{1,25},{9,1},{17,9},{25,17},{2,26},{10... | collective-permute-start | bytes 786440 | tf_op jit(solution)/shard_map/ppermute | solution.py:234
  86.2 4.1 %collective-permute-start.2 = (f32[2,64,512]{2,1,0:T(8,128)S(1)}, f32[2,64,512]{2,1,0:T(8,128)S(1)}, u32[]{:S(2)}, u32[]{:S(2)}) collective-permute-start(f32[2,64,512]{2,1,0:T(8,128)S(1)} %collective-permute-done.own), channel_id=1, source_target_pairs={{0,16},{8,24},{16,0},{24,8},{1,17},{9,25},{17,1},{25,9},{2,18},{10... | collective-permute-start | bytes 786440 | tf_op jit(solution)/shard_map/ppermute | solution.py:234
  90.4 3.9 %collective-permute-start.1 = (f32[2,64,512]{2,1,0:T(8,128)S(1)}, f32[2,64,512]{2,1,0:T(8,128)S(1)}, u32[]{:S(2)}, u32[]{:S(2)}) collective-permute-start(f32[2,64,512]{2,1,0:T(8,128)S(1)} %collective-permute-done.own), channel_id=1, source_target_pairs={{0,8},{8,16},{16,24},{24,0},{1,9},{9,17},{17,25},{25,1},{2,10},{10... | collective-permute-start | bytes 786440 | tf_op jit(solution)/shard_map/ppermute | solution.py:234
  94.3 0.7 copy-done.7
  95.0 8.8 %collective-permute-done.3.refs_2_.z3 = f32[2,64,512]{2,1,0:T(8,128)S(1)} collective-permute-done((f32[2,64,512]{2,1,0:T(8,128)S(1)}, f32[2,64,512]{2,1,0:T(8,128)S(1)}, u32[]{:S(2)}, u32[]{:S(2)}) %collective-permute-start.3) | collective-permute-done | bytes 262176 | tf_op jit(solution)/shard_map/ppermute | solution.py:234
  103.8 3.1 %collective-permute-done.2.refs_1_.z2 = f32[2,64,512]{2,1,0:T(8,128)S(1)} collective-permute-done((f32[2,64,512]{2,1,0:T(8,128)S(1)}, f32[2,64,512]{2,1,0:T(8,128)S(1)}, u32[]{:S(2)}, u32[]{:S(2)}) %collective-permute-start.2) | collective-permute-done | bytes 262176 | tf_op jit(solution)/shard_map/ppermute | solution.py:234
  106.9 2.0 %collective-permute-done.1.refs_0_.z1 = f32[2,64,512]{2,1,0:T(8,128)S(1)} collective-permute-done((f32[2,64,512]{2,1,0:T(8,128)S(1)}, f32[2,64,512]{2,1,0:T(8,128)S(1)}, u32[]{:S(2)}, u32[]{:S(2)}) %collective-permute-start.1) | collective-permute-done | bytes 262176 | tf_op jit(solution)/shard_map/ppermute | solution.py:234
  109.0 0.1 shard_map.31
  109.1 2.2 %collective-permute-start.6 = (f32[7,64,512]{2,1,0:T(8,128)S(1)}, f32[7,64,512]{2,1,0:T(8,128)S(1)}, u32[]{:S(2)}, u32[]{:S(2)}) collective-permute-start(f32[7,64,512]{2,1,0:T(8,128)S(1)} %get-tuple-element.16), channel_id=1, source_target_pairs={{0,32},{32,64},{64,96},{96,0},{1,33},{33,65},{65,97},{97,1},{2,34}... | collective-permute-start | bytes 2752520 | tf_op jit(solution)/shard_map/ppermute | solution.py:238
  111.3 4.9 %collective-permute-start.7 = (f32[7,64,512]{2,1,0:T(8,128)S(1)}, f32[7,64,512]{2,1,0:T(8,128)S(1)}, u32[]{:S(2)}, u32[]{:S(2)}) collective-permute-start(f32[7,64,512]{2,1,0:T(8,128)S(1)} %get-tuple-element.17), channel_id=1, source_target_pairs={{0,96},{32,0},{64,32},{96,64},{1,97},{33,1},{65,33},{97,65},{2,98}... | collective-permute-start | bytes 2752520 | tf_op jit(solution)/shard_map/ppermute | solution.py:239
  116.2 18.3 %collective-permute-done.6.up.refs_0_ = f32[7,64,512]{2,1,0:T(8,128)S(1)} collective-permute-done((f32[7,64,512]{2,1,0:T(8,128)S(1)}, f32[7,64,512]{2,1,0:T(8,128)S(1)}, u32[]{:S(2)}, u32[]{:S(2)}) %collective-permute-start.6) | collective-permute-done | bytes 917536 | tf_op jit(solution)/shard_map/ppermute | solution.py:238
  134.5 1.2 collective-permute-done.7.down.refs_1_
  135.7 0.9 shard_map.33
  136.6 2.7 %collective-permute-start.8 = (f32[3,64,512]{2,1,0:T(8,128)}, f32[3,64,512]{2,1,0:T(8,128)S(1)}, u32[]{:S(2)}, u32[]{:S(2)}) collective-permute-start(f32[3,64,512]{2,1,0:T(8,128)} %get-tuple-element.20), channel_id=1, source_target_pairs={{0,32},{32,64},{64,96},{96,0},{1,33},{33,65},{65,97},{97,1},{2,34}... | collective-permute-start | bytes 1179656 | tf_op jit(solution)/shard_map/ppermute | solution.py:241
  139.4 4.8 %collective-permute-start.9 = (f32[3,64,512]{2,1,0:T(8,128)}, f32[3,64,512]{2,1,0:T(8,128)S(1)}, u32[]{:S(2)}, u32[]{:S(2)}) collective-permute-start(f32[3,64,512]{2,1,0:T(8,128)} %get-tuple-element.21), channel_id=1, source_target_pairs={{0,96},{32,0},{64,32},{96,64},{1,97},{33,1},{65,33},{97,65},{2,98}... | collective-permute-start | bytes 1179656 | tf_op jit(solution)/shard_map/ppermute | solution.py:242
  144.2 0.1 pad_add_fusion.where
  144.2 0.9 copy-done.1
  145.2 0.9 copy-done.3
  146.1 1.6 copy-done.6
  147.7 0.9 copy-done.8
  148.7 4.9 %shard_map.32 = (f32[2,512,1024]{2,1,0:T(8,128)}, bf16[2,512,512]{2,1,0:T(8,128)(2,1)S(1)}, bf16[2,512,512]{2,1,0:T(8,128)(2,1)S(1)}) custom-call(s32[2]{0:T(128)S(1)} %pad_add_fusion.where, f32[8,2,64,512]{3,2,1,0:T(8,128)S(1)} %bitcast.7, f32[2,64,512]{2,1,0:T(8,128)S(1)} %copy-done.8, f32[2,64,512]{2,1,0:T(8,128)S(1)} %copy-done.3, ...), custom_call_target="tpu_custom_call" | custom-call | flops 2415919104 | bytes 3145728 | tf_op jit(solution)/shard_map/pallas_call | solution.py:173
  153.6 2.7 %shard_map.34 = f32[2,512,1024]{2,1,0:T(8,128)} custom-call(s32[2]{0:T(128)S(1)} %pad_add_fusion.where, bf16[2,512,512]{2,1,0:T(8,128)(2,1)S(1)} %get-tuple-element.18.row_high, bf16[2,512,512]{2,1,0:T(8,128)(2,1)S(1)} %get-tuple-element.19.row_low, f32[7,64,512]{2,1,0:T(8,128)S(1)} %collective-permute-done.6.up.refs_0_, ...), custom_call_target="tpu_custom_call", output_to_operand_aliasing={{}: (7, {})} | custom-call | flops 805306368 | bytes 1048576 | tf_op jit(solution)/shard_map/pallas_call | solution.py:195
  (19 shorter events, 0.1 us)
Async XLA Ops:
  6.5 137.7 %all-gather.3.cloned.1.call-start = ((), (), s32[]{:S(2)}) async-start(), calls=%async_computation.1 | async-start | bytes 2359296 | tf_op jit(solution)/shard_map/all_gather | solution.py:231
  6.5 0.9 copy-start.4
  7.5 0.9 copy-start.5
  61.8 16.6 %collective-permute-start = (f32[2,64,512]{2,1,0:T(8,128)}, f32[2,64,512]{2,1,0:T(8,128)S(1)}, u32[]{:S(2)}, u32[]{:S(2)}) collective-permute-start(f32[2,64,512]{2,1,0:T(8,128)} %shard_map.30), channel_id=1, source_target_pairs={{0,0},{1,8},{2,32},{3,40},{4,64},{5,72},{6,96},{7,104},{8,16},{9,2... | collective-permute-start | bytes 786440 | tf_op jit(solution)/shard_map/ppermute | solution.py:233
  78.4 16.6 %collective-permute-start.5 = (f32[2,64,512]{2,1,0:T(8,128)S(1)}, f32[2,64,512]{2,1,0:T(8,128)S(1)}, u32[]{:S(2)}, u32[]{:S(2)}) collective-permute-start(f32[2,64,512]{2,1,0:T(8,128)S(1)} %collective-permute-done.own), channel_id=1, source_target_pairs={{0,96},{32,0},{64,32},{96,64},{1,97},{33,1},{65,33},{97,65},{2,98}... | collective-permute-start | bytes 786440 | tf_op jit(solution)/shard_map/ppermute | solution.py:236
  80.4 14.6 %collective-permute-start.4 = (f32[2,64,512]{2,1,0:T(8,128)S(1)}, f32[2,64,512]{2,1,0:T(8,128)S(1)}, u32[]{:S(2)}, u32[]{:S(2)}) collective-permute-start(f32[2,64,512]{2,1,0:T(8,128)S(1)} %collective-permute-done.own), channel_id=1, source_target_pairs={{0,32},{32,64},{64,96},{96,0},{1,33},{33,65},{65,97},{97,1},{2,34}... | collective-permute-start | bytes 786440 | tf_op jit(solution)/shard_map/ppermute | solution.py:235
  84.3 19.5 %collective-permute-start.3 = (f32[2,64,512]{2,1,0:T(8,128)S(1)}, f32[2,64,512]{2,1,0:T(8,128)S(1)}, u32[]{:S(2)}, u32[]{:S(2)}) collective-permute-start(f32[2,64,512]{2,1,0:T(8,128)S(1)} %collective-permute-done.own), channel_id=1, source_target_pairs={{0,24},{8,0},{16,8},{24,16},{1,25},{9,1},{17,9},{25,17},{2,26},{10... | collective-permute-start | bytes 786440 | tf_op jit(solution)/shard_map/ppermute | solution.py:234
  86.2 20.7 %collective-permute-start.2 = (f32[2,64,512]{2,1,0:T(8,128)S(1)}, f32[2,64,512]{2,1,0:T(8,128)S(1)}, u32[]{:S(2)}, u32[]{:S(2)}) collective-permute-start(f32[2,64,512]{2,1,0:T(8,128)S(1)} %collective-permute-done.own), channel_id=1, source_target_pairs={{0,16},{8,24},{16,0},{24,8},{1,17},{9,25},{17,1},{25,9},{2,18},{10... | collective-permute-start | bytes 786440 | tf_op jit(solution)/shard_map/ppermute | solution.py:234
  90.4 18.6 %collective-permute-start.1 = (f32[2,64,512]{2,1,0:T(8,128)S(1)}, f32[2,64,512]{2,1,0:T(8,128)S(1)}, u32[]{:S(2)}, u32[]{:S(2)}) collective-permute-start(f32[2,64,512]{2,1,0:T(8,128)S(1)} %collective-permute-done.own), channel_id=1, source_target_pairs={{0,8},{8,16},{16,24},{24,0},{1,9},{9,17},{17,25},{25,1},{2,10},{10... | collective-permute-start | bytes 786440 | tf_op jit(solution)/shard_map/ppermute | solution.py:234
  94.3 0.7 copy-start.7
  106.9 32.4 %copy-start = (f32[2,64,512]{2,1,0:T(8,128)}, f32[2,64,512]{2,1,0:T(8,128)S(1)}, u32[]{:S(2)}) copy-start(f32[2,64,512]{2,1,0:T(8,128)S(1)} %collective-permute-done.2.refs_1_.z2) | copy-start | bytes 786436
  109.0 30.4 %copy-start.2 = (f32[2,64,512]{2,1,0:T(8,128)}, f32[2,64,512]{2,1,0:T(8,128)S(1)}, u32[]{:S(2)}) copy-start(f32[2,64,512]{2,1,0:T(8,128)S(1)} %collective-permute-done.1.refs_0_.z1) | copy-start | bytes 786436
  109.1 25.4 %collective-permute-start.6 = (f32[7,64,512]{2,1,0:T(8,128)S(1)}, f32[7,64,512]{2,1,0:T(8,128)S(1)}, u32[]{:S(2)}, u32[]{:S(2)}) collective-permute-start(f32[7,64,512]{2,1,0:T(8,128)S(1)} %get-tuple-element.16), channel_id=1, source_target_pairs={{0,32},{32,64},{64,96},{96,0},{1,33},{33,65},{65,97},{97,1},{2,34}... | collective-permute-start | bytes 2752520 | tf_op jit(solution)/shard_map/ppermute | solution.py:238
  111.3 24.3 %collective-permute-start.7 = (f32[7,64,512]{2,1,0:T(8,128)S(1)}, f32[7,64,512]{2,1,0:T(8,128)S(1)}, u32[]{:S(2)}, u32[]{:S(2)}) collective-permute-start(f32[7,64,512]{2,1,0:T(8,128)S(1)} %get-tuple-element.17), channel_id=1, source_target_pairs={{0,96},{32,0},{64,32},{96,64},{1,97},{33,1},{65,33},{97,65},{2,98}... | collective-permute-start | bytes 2752520 | tf_op jit(solution)/shard_map/ppermute | solution.py:239
  136.6 17.0 %collective-permute-start.8 = (f32[3,64,512]{2,1,0:T(8,128)}, f32[3,64,512]{2,1,0:T(8,128)S(1)}, u32[]{:S(2)}, u32[]{:S(2)}) collective-permute-start(f32[3,64,512]{2,1,0:T(8,128)} %get-tuple-element.20), channel_id=1, source_target_pairs={{0,32},{32,64},{64,96},{96,0},{1,33},{33,65},{65,97},{97,1},{2,34}... | collective-permute-start | bytes 1179656 | tf_op jit(solution)/shard_map/ppermute | solution.py:241
  139.4 14.2 %collective-permute-start.9 = (f32[3,64,512]{2,1,0:T(8,128)}, f32[3,64,512]{2,1,0:T(8,128)S(1)}, u32[]{:S(2)}, u32[]{:S(2)}) collective-permute-start(f32[3,64,512]{2,1,0:T(8,128)} %get-tuple-element.21), channel_id=1, source_target_pairs={{0,96},{32,0},{64,32},{96,64},{1,97},{33,1},{65,33},{97,65},{2,98}... | collective-permute-start | bytes 1179656 | tf_op jit(solution)/shard_map/ppermute | solution.py:242
  144.2 1.0 copy-start.1
  145.2 0.9 copy-start.3
  146.1 1.6 copy-start.6
  147.7 0.9 copy-start.8
Sparse Core Ops, SparseCore 0:
  62.0 28.0 all-gather.2

commit v2 on v1

--- a/solution.py
+++ b/solution.py
@@ -32,7 +32,11 @@
     return [(i, (i + step) % N) for i in range(N)]
 
 
-def local(kernel, shapes, *blocks, after=(), specs=None):
+def ring_pairs():
+    return [(y * 2 + core, (y + (1, N - 1)[core]) % N * 2 + core) for y in range(N) for core in range(2)]
+
+
+def local(kernel, shapes, *blocks, after=(), specs=None, scratch=()):
     skip = len(after)
 
     def run(*refs):
@@ -44,12 +48,21 @@
         in_specs=(specs or [WHOLE] * len(blocks)) + [pl.BlockSpec(memory_space=pl.ANY)] * skip,
         out_specs=[WHOLE] * len(shapes),
         out_shape=shapes,
+        scratch_shapes=scratch,
         compiler_params=pltpu.CompilerParams(vmem_limit_bytes=8 * 1024 * 1024),
         cost_estimate=pl.CostEstimate(flops=moved, bytes_accessed=moved, transcendentals=0),
     )(*blocks, *after)
 
 
-def sums_kernel(returns, traded, masked, sums):
+def sums_kernel(returns_far, traded_far, masked, sums, returns, traded, sems):
+    copies = [
+        pltpu.make_async_copy(returns_far, returns, sems.at[0]),
+        pltpu.make_async_copy(traded_far, traded, sems.at[1]),
+    ]
+    for copy in copies:
+        copy.start()
+    for copy in copies:
+        copy.wait()
     share = sums.shape[2]
     for group in range(N):
         rows = slice(group * share, (group + 1) * share)
@@ -78,19 +91,9 @@
         scaled[k] = masked[k] * weight[...]
 
 
-def pack_kernel(z1, z2, z3, y_up, y_down, up, down):
-    for n, piece in enumerate((z1, z2, z3)):
-        for k in range(2):
-            up[2 * n + k] = piece[k]
-            down[2 * n + k] = piece[k]
-    up[6] = y_up[0]
-    down[6] = y_down[1]
-
-
-def hand_on_kernel(from_up, from_down, up, down):
-    for n, (here, there) in enumerate(((0, 4), (1, 5), (2, 3))):
-        up[n] = from_up[here]
-        down[n] = from_down[there]
+def pair_kernel(first, second, out):
+    out[:2] = first[...]
+    out[2:] = second[...]
 
 
 def split(value):
@@ -115,7 +118,7 @@
 
 def send_columns(where, step, k, tile, out, sems):
     half = tile.shape[1] // 2
-    x = lax.rem(where[0] - step + N, N)
+    x = lax.rem(where[0] + step * where[2], N)
     copies = []
     for p in range(2):
         start = pl.multiple_of((p * N + x) * half, half)
@@ -126,7 +129,7 @@
 
 
 def near_kernel(
-    where, rows, own, z1, z2, z3, y_up, up, y_down, down, out, row_high, row_low, high, low, tiles, sems
+    where, rows, a, b, a_one, b_one, a_two, b_two, out, row_high, row_low, high, low, tiles, sems
 ):
     size = rows.shape[2]
     copies = []
@@ -134,32 +137,24 @@
         for n in range(rows.shape[0]):
             part = slice(n * size, (n + 1) * size)
             row_high[k, part, :], row_low[k, part, :] = split(rows[n, k])
-        groups = (
-            (0, [own[k], z1[k], z2[k], z3[k]]),
-            (1, [y_up[k], up[k], up[2 + k], up[4 + k]]),
-            (3, [y_down[k], down[k], down[2 + k], down[4 + k]]),
-        )
-        for n, (step, blocks) in enumerate(groups):
-            spot = 3 * k + n
+        for step, (here, there) in enumerate(((a, b), (a_one, b_one), (a_two, b_two))):
+            blocks = [there[k], there[2 + k], here[k], here[2 + k]]
+            spot = 3 * k + step
             keep_columns(where, spot, blocks, high, low)
-            tiles[k, n] = triple(row_high[k], row_low[k], high[spot], low[spot])
-            for copy in send_columns(where, step, k, tiles.at[k, n], out, sems.at[k, n]):
+            tiles[k, step] = triple(row_high[k], row_low[k], high[spot], low[spot])
+            for copy in send_columns(where, step, k, tiles.at[k, step], out, sems.at[k, step]):
                 copy.start()
                 copies.append(copy)
     for copy in copies:
         copy.wait()
 
 
-def far_kernel(where, row_high, row_low, up, down, far_up, far_down, kept, out, high, low, tiles, sems):
-    blocks = (
-        [up[6], far_up[0], far_up[2], far_down[0]],
-        [down[6], far_up[1], far_down[2], far_down[1]],
-    )
+def far_kernel(where, row_high, row_low, a, b, kept, out, high, low, tiles, sems):
     copies = []
     for k in range(2):
-        keep_columns(where, k, blocks[k], high, low)
+        keep_columns(where, k, [b[k], b[2 + k], a[k], a[2 + k]], high, low)
         tiles[k] = triple(row_high[k], row_low[k], high[k], low[k])
-        for copy in send_columns(where, 2, k, tiles.at[k], out, sems.at[k]):
+        for copy in send_columns(where, 3, k, tiles.at[k], out, sems.at[k]):
             copy.start()
             copies.append(copy)
     for copy in copies:
@@ -188,16 +183,16 @@
     )(where, rows, *blocks)
 
 
-def far_product(where, row_high, row_low, up, down, far_up, far_down, kept):
+def far_product(where, row_high, row_low, a, b, kept):
     days, height, bins = row_high.shape
     width = kept.shape[2] // N
     anywhere = pl.BlockSpec(memory_space=pl.ANY)
     return pl.pallas_call(
         far_kernel,
-        in_specs=[SCALARS] + [WHOLE] * 6 + [anywhere],
+        in_specs=[SCALARS] + [WHOLE] * 4 + [anywhere],
         out_specs=anywhere,
         out_shape=jax.ShapeDtypeStruct(kept.shape, kept.dtype),
-        input_output_aliases={7: 0},
+        input_output_aliases={5: 0},
         scratch_shapes=[
             pltpu.VMEM((days, width, bins), jnp.bfloat16),
             pltpu.VMEM((days, width, bins), jnp.bfloat16),
@@ -208,7 +203,7 @@
         cost_estimate=pl.CostEstimate(
             flops=6 * days * height * width * bins, bytes_accessed=4 * days * height * width, transcendentals=0
         ),
-    )(where, row_high, row_low, up, down, far_up, far_down, kept)
+    )(where, row_high, row_low, a, b, kept)
 
 
 def body(returns, traded):
@@ -221,7 +216,16 @@
         return jax.ShapeDtypeStruct(sizes, jnp.float32)
 
     masked, sums = local(
-        sums_kernel, [shape(days, size, bins), shape(N, 2, share, bins)], returns, traded, specs=[pl.BlockSpec()] * 2
+        sums_kernel,
+        [shape(days, size, bins), shape(N, 2, share, bins)],
+        returns,
+        traded,
+        specs=[pl.BlockSpec(memory_space=pltpu.HBM)] * 2,
+        scratch=[
+            pltpu.VMEM((days, size, bins), jnp.float32),
+            pltpu.VMEM((days, size, bins), jnp.int32),
+            pltpu.SemaphoreType.DMA((2,)),
+        ],
     )
     sums = lax.all_to_all(sums, DAY, 0, 0)
     (weight,) = local(weight_kernel, [shape(share, bins)], sums)
@@ -231,19 +235,17 @@
     rows = lax.all_gather(scaled, (X, CORE))
 
     turned = lax.ppermute(scaled, GROUP, turn_pairs())
-    z_pieces = [lax.ppermute(turned, Z, shift(step)) for step in (1, 2, 3)]
-    y_up = lax.ppermute(turned, Y, shift(1))
-    y_down = lax.ppermute(turned, Y, shift(-1))
-    up, down = local(pack_kernel, [shape(7, size, bins)] * 2, *z_pieces, y_up, y_down)
-    up = lax.ppermute(up, Y, shift(1))
-    down = lax.ppermute(down, Y, shift(-1))
-    far_up, far_down = local(hand_on_kernel, [shape(3, size, bins)] * 2, up, down)
-    far_up = lax.ppermute(far_up, Y, shift(1))
-    far_down = lax.ppermute(far_down, Y, shift(-1))
-
-    where = jnp.stack([lax.axis_index(Y), lax.axis_index(Z)]).astype(jnp.int32)
-    out, row_high, row_low = near_product(where, rows, turned, *z_pieces, y_up, up, y_down, down)
-    return far_product(where, row_high, row_low, up, down, far_up, far_down, out)
+    z1, z2, z3 = [lax.ppermute(turned, Z, shift(step)) for step in (1, 2, 3)]
+    (b,) = local(pair_kernel, [shape(4, size, bins)], turned, z1)
+    (a,) = local(pair_kernel, [shape(4, size, bins)], z2, z3)
+    units = [a, b]
+    for _ in range(N - 1):
+        units += [lax.ppermute(unit, (Y, CORE), ring_pairs()) for unit in units[-2:]]
+
+    back = lax.select(lax.axis_index(CORE) == 0, N - 1, 1)
+    where = jnp.stack([lax.axis_index(Y), lax.axis_index(Z), back]).astype(jnp.int32)
+    out, row_high, row_low = near_product(where, rows, *units[:6])
+    return far_product(where, row_high, row_low, *units[6:], out)
 
 
 def solution(mesh):

time: 164 us -> 154 us (0.939)
  the two profiles are of different devices: /device:TPU:68 before, /device:TPU:36 now
where the time goes in v2:
time: 154 us; the launch traced here: 153 us
  blocking collectives  52.7 us (34%)
  waiting for transfers between devices  45.2 us (29%)
  starting transfers between devices  28.6 us (19%)
  between operations  13.5 us (9%)
  Pallas kernels  9.28 us (6%)
  local copies, waits for them, and re-layouts  3.49 us (2%)
    all_to_all x1, blocking collectives, body(): sums = lax.all_to_all(sums, DAY, 0, 0)  35.3 us
    ppermute x6, waiting for transfers between devices, body(): lax.ppermute(unit, (Y, CORE), ring_pairs())  20.3 us
    all_gather x1, blocking collectives, body(): weight = lax.all_gather(weight, DAY, axis=0, tiled=True)  17.4 us
    ppermute x3, waiting for transfers between devices, body(): z1, z2, z3 = [lax.ppermute(turned, Z, shift(step)) for step in (1, 2, 3)]  15 us
    ppermute x6, starting transfers between devices, body(): lax.ppermute(unit, (Y, CORE), ring_pairs())  11.5 us
    ppermute x3, starting transfers between devices, body(): z1, z2, z3 = [lax.ppermute(turned, Z, shift(step)) for step in (1, 2, 3)]  11 us
    ppermute x1, waiting for transfers between devices, body(): turned = lax.ppermute(scaled, GROUP, turn_pairs())  9.98 us
    ppermute x1, starting transfers between devices, body(): turned = lax.ppermute(scaled, GROUP, turn_pairs())  6.16 us
  transfers between devices with their start and end apart: 11, of which 9 were waited for; matrix products, arithmetic and copies ran while one was open for 0% of the time, Pallas kernels for 4%

profile of v2, /device:TPU:36, one launch (start us, length us, event | category | flops | bytes accessed | tf_op | source)
XLA Modules:
  0.0 153.0 jit_solution(10039450350215066373)
XLA Ops:
  6.5 0.9 copy-done
  7.5 0.9 copy-done.1
  8.4 0.1 shard_map.28
  8.5 35.3 %all_to_all.5.refs_0_ = f32[4,2,16,512]{3,2,1,0:T(8,128)S(1)} all-to-all(f32[4,2,16,512]{3,2,1,0:T(8,128)S(1)} %get-tuple-element.11), channel_id=1, replica_groups=mesh['day'=4,'y'=4,'z'=4,'x'=4,'core'=2] {'day'}, dimensions={0} | all-to-all | bytes 524288 | tf_op jit(solution)/shard_map/all_to_all | solution.py:230
  43.8 0.1 shard_map.29
  43.9 17.4 %all_gather.9.refs_1_ = f32[64,512]{1,0:T(8,128)S(1)} all-gather(f32[16,512]{1,0:T(8,128)S(1)} %shard_map.29), channel_id=1, replica_groups=mesh['day'=4,'y'=4,'z'=4,'x'=4,'core'=2] {'day'}, dimensions={0}, use_global_device_ids=true | all-gather | bytes 163840 | tf_op jit(solution)/shard_map/all_gather | solution.py:232
  61.4 0.7 shard_map.30
  62.1 0.0 all-gather.3.cloned.1.call-update
  62.1 6.2 %collective-permute-start = (f32[2,64,512]{2,1,0:T(8,128)}, f32[2,64,512]{2,1,0:T(8,128)S(1)}, u32[]{:S(2)}, u32[]{:S(2)}) collective-permute-start(f32[2,64,512]{2,1,0:T(8,128)} %shard_map.30), channel_id=1, source_target_pairs={{0,0},{1,8},{2,32},{3,40},{4,64},{5,72},{6,96},{7,104},{8,16},{9,2... | collective-permute-start | bytes 786440 | tf_op jit(solution)/shard_map/ppermute | solution.py:237
  68.3 10.0 %collective-permute-done.refs_0_ = f32[2,64,512]{2,1,0:T(8,128)S(1)} collective-permute-done((f32[2,64,512]{2,1,0:T(8,128)}, f32[2,64,512]{2,1,0:T(8,128)S(1)}, u32[]{:S(2)}, u32[]{:S(2)}) %collective-permute-start) | collective-permute-done | bytes 262176 | tf_op jit(solution)/shard_map/ppermute | solution.py:237
  78.3 4.0 %collective-permute-start.3 = (f32[2,64,512]{2,1,0:T(8,128)S(1)}, f32[2,64,512]{2,1,0:T(8,128)S(1)}, u32[]{:S(2)}, u32[]{:S(2)}) collective-permute-start(f32[2,64,512]{2,1,0:T(8,128)S(1)} %collective-permute-done.refs_0_), channel_id=1, source_target_pairs={{0,8},{8,16},{16,24},{24,0},{1,9},{9,17},{17,25},{25,1},{2,10},{10... | collective-permute-start | bytes 786440 | tf_op jit(solution)/shard_map/ppermute | solution.py:238
  82.3 5.1 %collective-permute-start.1 = (f32[2,64,512]{2,1,0:T(8,128)S(1)}, f32[2,64,512]{2,1,0:T(8,128)S(1)}, u32[]{:S(2)}, u32[]{:S(2)}) collective-permute-start(f32[2,64,512]{2,1,0:T(8,128)S(1)} %collective-permute-done.refs_0_), channel_id=1, source_target_pairs={{0,16},{8,24},{16,0},{24,8},{1,17},{9,25},{17,1},{25,9},{2,18},{10... | collective-permute-start | bytes 786440 | tf_op jit(solution)/shard_map/ppermute | solution.py:238
  87.4 1.9 %collective-permute-start.2 = (f32[2,64,512]{2,1,0:T(8,128)S(1)}, f32[2,64,512]{2,1,0:T(8,128)S(1)}, u32[]{:S(2)}, u32[]{:S(2)}) collective-permute-start(f32[2,64,512]{2,1,0:T(8,128)S(1)} %collective-permute-done.refs_0_), channel_id=1, source_target_pairs={{0,24},{8,0},{16,8},{24,16},{1,25},{9,1},{17,9},{25,17},{2,26},{10... | collective-permute-start | bytes 786440 | tf_op jit(solution)/shard_map/ppermute | solution.py:238
  89.3 10.2 %collective-permute-done.3.refs_1_ = f32[2,64,512]{2,1,0:T(8,128)S(1)} collective-permute-done((f32[2,64,512]{2,1,0:T(8,128)S(1)}, f32[2,64,512]{2,1,0:T(8,128)S(1)}, u32[]{:S(2)}, u32[]{:S(2)}) %collective-permute-start.3) | collective-permute-done | bytes 262176 | tf_op jit(solution)/shard_map/ppermute | solution.py:238
  99.5 1.9 %collective-permute-start.5 = (f32[4,64,512]{2,1,0:T(8,128)S(1)}, f32[4,64,512]{2,1,0:T(8,128)S(1)}, u32[]{:S(2)}, u32[]{:S(2)}) collective-permute-start(f32[4,64,512]{2,1,0:T(8,128)S(1)} %shard_map.32.b), channel_id=1, source_target_pairs={{0,32},{1,97},{32,64},{33,1},{64,96},{65,33},{96,0},{97,65},{2,34}... | collective-permute-start | bytes 1572872 | tf_op jit(solution)/shard_map/ppermute | solution.py:243
  101.4 1.6 %collective-permute-done.1.refs_0_ = f32[2,64,512]{2,1,0:T(8,128)S(1)} collective-permute-done((f32[2,64,512]{2,1,0:T(8,128)S(1)}, f32[2,64,512]{2,1,0:T(8,128)S(1)}, u32[]{:S(2)}, u32[]{:S(2)}) %collective-permute-start.1) | collective-permute-done | bytes 262176 | tf_op jit(solution)/shard_map/ppermute | solution.py:238
  103.0 3.2 %collective-permute-done.2.refs_1_ = f32[2,64,512]{2,1,0:T(8,128)S(1)} collective-permute-done((f32[2,64,512]{2,1,0:T(8,128)S(1)}, f32[2,64,512]{2,1,0:T(8,128)S(1)}, u32[]{:S(2)}, u32[]{:S(2)}) %collective-permute-start.2) | collective-permute-done | bytes 262176 | tf_op jit(solution)/shard_map/ppermute | solution.py:238
  106.3 1.9 %collective-permute-start.4 = (f32[4,64,512]{2,1,0:T(8,128)S(1)}, f32[4,64,512]{2,1,0:T(8,128)S(1)}, u32[]{:S(2)}, u32[]{:S(2)}) collective-permute-start(f32[4,64,512]{2,1,0:T(8,128)S(1)} %shard_map.31.a), channel_id=1, source_target_pairs={{0,32},{1,97},{32,64},{33,1},{64,96},{65,33},{96,0},{97,65},{2,34}... | collective-permute-start | bytes 1572872 | tf_op jit(solution)/shard_map/ppermute | solution.py:243
  108.2 3.6 %collective-permute-done.5.b_one = f32[4,64,512]{2,1,0:T(8,128)S(1)} collective-permute-done((f32[4,64,512]{2,1,0:T(8,128)S(1)}, f32[4,64,512]{2,1,0:T(8,128)S(1)}, u32[]{:S(2)}, u32[]{:S(2)}) %collective-permute-start.5) | collective-permute-done | bytes 524320 | tf_op jit(solution)/shard_map/ppermute | solution.py:243
  111.8 1.9 %collective-permute-start.7 = (f32[4,64,512]{2,1,0:T(8,128)S(1)}, f32[4,64,512]{2,1,0:T(8,128)}, u32[]{:S(2)}, u32[]{:S(2)}) collective-permute-start(f32[4,64,512]{2,1,0:T(8,128)S(1)} %collective-permute-done.5.b_one), channel_id=1, source_target_pairs={{0,32},{1,97},{32,64},{33,1},{64,96},{65,33},{96,0},{97,65},{2,34}... | collective-permute-start | bytes 1572872 | tf_op jit(solution)/shard_map/ppermute | solution.py:243
  113.7 4.8 %collective-permute-done.4.a_one = f32[4,64,512]{2,1,0:T(8,128)S(1)} collective-permute-done((f32[4,64,512]{2,1,0:T(8,128)S(1)}, f32[4,64,512]{2,1,0:T(8,128)S(1)}, u32[]{:S(2)}, u32[]{:S(2)}) %collective-permute-start.4) | collective-permute-done | bytes 524320 | tf_op jit(solution)/shard_map/ppermute | solution.py:243
  118.6 1.9 %collective-permute-start.6 = (f32[4,64,512]{2,1,0:T(8,128)S(1)}, f32[4,64,512]{2,1,0:T(8,128)}, u32[]{:S(2)}, u32[]{:S(2)}) collective-permute-start(f32[4,64,512]{2,1,0:T(8,128)S(1)} %collective-permute-done.4.a_one), channel_id=1, source_target_pairs={{0,32},{1,97},{32,64},{33,1},{64,96},{65,33},{96,0},{97,65},{2,34}... | collective-permute-start | bytes 1572872 | tf_op jit(solution)/shard_map/ppermute | solution.py:243
  120.5 3.8 %collective-permute-done.7.b_two = f32[4,64,512]{2,1,0:T(8,128)} collective-permute-done((f32[4,64,512]{2,1,0:T(8,128)S(1)}, f32[4,64,512]{2,1,0:T(8,128)}, u32[]{:S(2)}, u32[]{:S(2)}) %collective-permute-start.7) | collective-permute-done | bytes 524320 | tf_op jit(solution)/shard_map/ppermute | solution.py:243
  124.3 1.9 %collective-permute-start.9 = (f32[4,64,512]{2,1,0:T(8,128)}, f32[4,64,512]{2,1,0:T(8,128)S(1)}, u32[]{:S(2)}, u32[]{:S(2)}) collective-permute-start(f32[4,64,512]{2,1,0:T(8,128)} %collective-permute-done.7.b_two), channel_id=1, source_target_pairs={{0,32},{1,97},{32,64},{33,1},{64,96},{65,33},{96,0},{97,65},{2,34}... | collective-permute-start | bytes 1572872 | tf_op jit(solution)/shard_map/ppermute | solution.py:243
  126.2 4.7 %collective-permute-done.6.a_two = f32[4,64,512]{2,1,0:T(8,128)} collective-permute-done((f32[4,64,512]{2,1,0:T(8,128)S(1)}, f32[4,64,512]{2,1,0:T(8,128)}, u32[]{:S(2)}, u32[]{:S(2)}) %collective-permute-start.6) | collective-permute-done | bytes 524320 | tf_op jit(solution)/shard_map/ppermute | solution.py:243
  130.9 1.9 %collective-permute-start.8 = (f32[4,64,512]{2,1,0:T(8,128)}, f32[4,64,512]{2,1,0:T(8,128)S(1)}, u32[]{:S(2)}, u32[]{:S(2)}) collective-permute-start(f32[4,64,512]{2,1,0:T(8,128)} %collective-permute-done.6.a_two), channel_id=1, source_target_pairs={{0,32},{1,97},{32,64},{33,1},{64,96},{65,33},{96,0},{97,65},{2,34}... | collective-permute-start | bytes 1572872 | tf_op jit(solution)/shard_map/ppermute | solution.py:243
  132.9 0.1 pad_add_fusion.where
  132.9 1.6 %copy-done.2 = f32[16,64,512]{2,1,0:T(8,128)S(1)} copy-done((f32[16,64,512]{2,1,0:T(8,128)S(1)}, f32[16,64,512]{2,1,0:T(8,128)}, u32[]{:S(2)}) %copy-start.2) | copy-done | bytes 2097176
  134.5 5.6 %shard_map.33 = (f32[2,512,1024]{2,1,0:T(8,128)}, bf16[2,512,512]{2,1,0:T(8,128)(2,1)S(1)}, bf16[2,512,512]{2,1,0:T(8,128)(2,1)S(1)}) custom-call(s32[3]{0:T(128)S(1)} %pad_add_fusion.where, f32[8,2,64,512]{3,2,1,0:T(8,128)S(1)} %bitcast.8, f32[4,64,512]{2,1,0:T(8,128)S(1)} %shard_map.31.a, f32[4,64,512]{2,1,0:T(8,128)S(1)} %shard_map.32.b, ...), custom_call_target="tpu_custom_call" | custom-call | flops 2415919104 | bytes 3145728 | tf_op jit(solution)/shard_map/pallas_call | solution.py:168
  140.1 0.0 collective-permute-done.9.b
  140.1 3.3 %collective-permute-done.8.a = f32[4,64,512]{2,1,0:T(8,128)S(1)} collective-permute-done((f32[4,64,512]{2,1,0:T(8,128)}, f32[4,64,512]{2,1,0:T(8,128)S(1)}, u32[]{:S(2)}, u32[]{:S(2)}) %collective-permute-start.8) | collective-permute-done | bytes 524320 | tf_op jit(solution)/shard_map/ppermute | solution.py:243
  143.4 2.7 %shard_map.34 = f32[2,512,1024]{2,1,0:T(8,128)} custom-call(s32[3]{0:T(128)S(1)} %pad_add_fusion.where, bf16[2,512,512]{2,1,0:T(8,128)(2,1)S(1)} %get-tuple-element.12.row_high, bf16[2,512,512]{2,1,0:T(8,128)(2,1)S(1)} %get-tuple-element.13.row_low, f32[4,64,512]{2,1,0:T(8,128)S(1)} %collective-permute-done.8.a, ...), custom_call_target="tpu_custom_call", output_to_operand_aliasing={{}: (5, {})} | custom-call | flops 805306368 | bytes 1048576 | tf_op jit(solution)/shard_map/pallas_call | solution.py:190
  (7 shorter events, 0.1 us)
Async XLA Ops:
  6.5 126.4 %all-gather.3.cloned.1.call-start = ((), (), s32[]{:S(2)}) async-start(), calls=%async_computation.1 | async-start | bytes 2359296 | tf_op jit(solution)/shard_map/all_gather | solution.py:235
  6.5 0.9 copy-start
  7.5 0.9 copy-start.1
  62.1 16.1 %collective-permute-start = (f32[2,64,512]{2,1,0:T(8,128)}, f32[2,64,512]{2,1,0:T(8,128)S(1)}, u32[]{:S(2)}, u32[]{:S(2)}) collective-permute-start(f32[2,64,512]{2,1,0:T(8,128)} %shard_map.30), channel_id=1, source_target_pairs={{0,0},{1,8},{2,32},{3,40},{4,64},{5,72},{6,96},{7,104},{8,16},{9,2... | collective-permute-start | bytes 786440 | tf_op jit(solution)/shard_map/ppermute | solution.py:237
  78.3 21.2 %collective-permute-start.3 = (f32[2,64,512]{2,1,0:T(8,128)S(1)}, f32[2,64,512]{2,1,0:T(8,128)S(1)}, u32[]{:S(2)}, u32[]{:S(2)}) collective-permute-start(f32[2,64,512]{2,1,0:T(8,128)S(1)} %collective-permute-done.refs_0_), channel_id=1, source_target_pairs={{0,8},{8,16},{16,24},{24,0},{1,9},{9,17},{17,25},{25,1},{2,10},{10... | collective-permute-start | bytes 786440 | tf_op jit(solution)/shard_map/ppermute | solution.py:238
  82.3 20.7 %collective-permute-start.1 = (f32[2,64,512]{2,1,0:T(8,128)S(1)}, f32[2,64,512]{2,1,0:T(8,128)S(1)}, u32[]{:S(2)}, u32[]{:S(2)}) collective-permute-start(f32[2,64,512]{2,1,0:T(8,128)S(1)} %collective-permute-done.refs_0_), channel_id=1, source_target_pairs={{0,16},{8,24},{16,0},{24,8},{1,17},{9,25},{17,1},{25,9},{2,18},{10... | collective-permute-start | bytes 786440 | tf_op jit(solution)/shard_map/ppermute | solution.py:238
  87.4 18.9 %collective-permute-start.2 = (f32[2,64,512]{2,1,0:T(8,128)S(1)}, f32[2,64,512]{2,1,0:T(8,128)S(1)}, u32[]{:S(2)}, u32[]{:S(2)}) collective-permute-start(f32[2,64,512]{2,1,0:T(8,128)S(1)} %collective-permute-done.refs_0_), channel_id=1, source_target_pairs={{0,24},{8,0},{16,8},{24,16},{1,25},{9,1},{17,9},{25,17},{2,26},{10... | collective-permute-start | bytes 786440 | tf_op jit(solution)/shard_map/ppermute | solution.py:238
  99.5 12.3 %collective-permute-start.5 = (f32[4,64,512]{2,1,0:T(8,128)S(1)}, f32[4,64,512]{2,1,0:T(8,128)S(1)}, u32[]{:S(2)}, u32[]{:S(2)}) collective-permute-start(f32[4,64,512]{2,1,0:T(8,128)S(1)} %shard_map.32.b), channel_id=1, source_target_pairs={{0,32},{1,97},{32,64},{33,1},{64,96},{65,33},{96,0},{97,65},{2,34}... | collective-permute-start | bytes 1572872 | tf_op jit(solution)/shard_map/ppermute | solution.py:243
  106.3 12.3 %collective-permute-start.4 = (f32[4,64,512]{2,1,0:T(8,128)S(1)}, f32[4,64,512]{2,1,0:T(8,128)S(1)}, u32[]{:S(2)}, u32[]{:S(2)}) collective-permute-start(f32[4,64,512]{2,1,0:T(8,128)S(1)} %shard_map.31.a), channel_id=1, source_target_pairs={{0,32},{1,97},{32,64},{33,1},{64,96},{65,33},{96,0},{97,65},{2,34}... | collective-permute-start | bytes 1572872 | tf_op jit(solution)/shard_map/ppermute | solution.py:243
  111.8 12.5 %collective-permute-start.7 = (f32[4,64,512]{2,1,0:T(8,128)S(1)}, f32[4,64,512]{2,1,0:T(8,128)}, u32[]{:S(2)}, u32[]{:S(2)}) collective-permute-start(f32[4,64,512]{2,1,0:T(8,128)S(1)} %collective-permute-done.5.b_one), channel_id=1, source_target_pairs={{0,32},{1,97},{32,64},{33,1},{64,96},{65,33},{96,0},{97,65},{2,34}... | collective-permute-start | bytes 1572872 | tf_op jit(solution)/shard_map/ppermute | solution.py:243
  118.6 12.4 %collective-permute-start.6 = (f32[4,64,512]{2,1,0:T(8,128)S(1)}, f32[4,64,512]{2,1,0:T(8,128)}, u32[]{:S(2)}, u32[]{:S(2)}) collective-permute-start(f32[4,64,512]{2,1,0:T(8,128)S(1)} %collective-permute-done.4.a_one), channel_id=1, source_target_pairs={{0,32},{1,97},{32,64},{33,1},{64,96},{65,33},{96,0},{97,65},{2,34}... | collective-permute-start | bytes 1572872 | tf_op jit(solution)/shard_map/ppermute | solution.py:243
  124.3 15.8 %collective-permute-start.9 = (f32[4,64,512]{2,1,0:T(8,128)}, f32[4,64,512]{2,1,0:T(8,128)S(1)}, u32[]{:S(2)}, u32[]{:S(2)}) collective-permute-start(f32[4,64,512]{2,1,0:T(8,128)} %collective-permute-done.7.b_two), channel_id=1, source_target_pairs={{0,32},{1,97},{32,64},{33,1},{64,96},{65,33},{96,0},{97,65},{2,34}... | collective-permute-start | bytes 1572872 | tf_op jit(solution)/shard_map/ppermute | solution.py:243
  130.9 12.5 %collective-permute-start.8 = (f32[4,64,512]{2,1,0:T(8,128)}, f32[4,64,512]{2,1,0:T(8,128)S(1)}, u32[]{:S(2)}, u32[]{:S(2)}) collective-permute-start(f32[4,64,512]{2,1,0:T(8,128)} %collective-permute-done.6.a_two), channel_id=1, source_target_pairs={{0,32},{1,97},{32,64},{33,1},{64,96},{65,33},{96,0},{97,65},{2,34}... | collective-permute-start | bytes 1572872 | tf_op jit(solution)/shard_map/ppermute | solution.py:243
  132.9 1.6 %copy-start.2 = (f32[16,64,512]{2,1,0:T(8,128)S(1)}, f32[16,64,512]{2,1,0:T(8,128)}, u32[]{:S(2)}) copy-start(f32[16,64,512]{2,1,0:T(8,128)} %all-gather.3.cloned.1.call-done) | copy-start | bytes 6291460
Sparse Core Ops, SparseCore 0:
  62.3 28.1 all-gather.2

commit v3 on v2

--- a/solution.py
+++ b/solution.py
@@ -36,7 +36,7 @@
     return [(y * 2 + core, (y + (1, N - 1)[core]) % N * 2 + core) for y in range(N) for core in range(2)]
 
 
-def local(kernel, shapes, *blocks, after=(), specs=None, scratch=()):
+def local(kernel, shapes, *blocks, after=(), specs=None, scratch=(), limit=8):
     skip = len(after)
 
     def run(*refs):
@@ -49,7 +49,7 @@
         out_specs=[WHOLE] * len(shapes),
         out_shape=shapes,
         scratch_shapes=scratch,
-        compiler_params=pltpu.CompilerParams(vmem_limit_bytes=8 * 1024 * 1024),
+        compiler_params=pltpu.CompilerParams(vmem_limit_bytes=limit * 1024 * 1024),
         cost_estimate=pl.CostEstimate(flops=moved, bytes_accessed=moved, transcendentals=0),
     )(*blocks, *after)
 
@@ -226,15 +226,17 @@
             pltpu.VMEM((days, size, bins), jnp.int32),
             pltpu.SemaphoreType.DMA((2,)),
         ],
+        limit=60,
     )
     sums = lax.all_to_all(sums, DAY, 0, 0)
     (weight,) = local(weight_kernel, [shape(share, bins)], sums)
     weight = lax.all_gather(weight, DAY, axis=0, tiled=True)
     (scaled,) = local(scale_kernel, [shape(days, size, bins)], masked, weight)
 
-    rows = lax.all_gather(scaled, (X, CORE))
-
     turned = lax.ppermute(scaled, GROUP, turn_pairs())
+
+    rows = lax.all_gather(lax.optimization_barrier((scaled, turned))[0], (X, CORE))
+
     z1, z2, z3 = [lax.ppermute(turned, Z, shift(step)) for step in (1, 2, 3)]
     (b,) = local(pair_kernel, [shape(4, size, bins)], turned, z1)
     (a,) = local(pair_kernel, [shape(4, size, bins)], z2, z3)

time: 154 us -> 155 us (level)
  Pallas kernels: 9.28 us -> 11.1 us
    pallas_call x5, Pallas kernels: 1.01 us -> 2.78 us  [local(): pl.pallas_call(run, in_specs=(specs or [WHOLE] * len(blocks)) + [pl.Block...]
    unnamed x6 -> x4, local copies, waits for them, and re-layouts: 3.49 us -> 2.54 us
where the time goes in v3:
time: 155 us; the launch traced here: 154 us
  blocking collectives  52.9 us (34%)
  waiting for transfers between devices  45.2 us (29%)
  starting transfers between devices  28.6 us (18%)
  between operations  13.5 us (9%)
  Pallas kernels  11.1 us (7%)
  local copies, waits for them, and re-layouts  2.54 us (2%)
    all_to_all x1, blocking collectives, body(): sums = lax.all_to_all(sums, DAY, 0, 0)  35.5 us
    ppermute x6, waiting for transfers between devices, body(): lax.ppermute(unit, (Y, CORE), ring_pairs())  20.3 us
    all_gather x1, blocking collectives, body(): weight = lax.all_gather(weight, DAY, axis=0, tiled=True)  17.4 us
    ppermute x3, waiting for transfers between devices, body(): z1, z2, z3 = [lax.ppermute(turned, Z, shift(step)) for step in (1, 2, 3)]  15 us
    ppermute x6, starting transfers between devices, body(): lax.ppermute(unit, (Y, CORE), ring_pairs())  11.5 us
    ppermute x3, starting transfers between devices, body(): z1, z2, z3 = [lax.ppermute(turned, Z, shift(step)) for step in (1, 2, 3)]  11 us
    ppermute x1, waiting for transfers between devices, body(): turned = lax.ppermute(scaled, GROUP, turn_pairs())  9.98 us
    ppermute x1, starting transfers between devices, body(): turned = lax.ppermute(scaled, GROUP, turn_pairs())  6.15 us
  transfers between devices with their start and end apart: 11, of which 9 were waited for; matrix products, arithmetic and copies ran while one was open for 0% of the time, Pallas kernels for 4%

profile of v3, /device:TPU:36, one launch (start us, length us, event | category | flops | bytes accessed | tf_op | source)
XLA Modules:
  0.0 154.0 jit_solution(14827416757686658006)
XLA Ops:
  6.5 0.0 all-gather.3.cloned.1.call-start
  6.5 1.9 %shard_map.28 = (f32[2,64,512]{2,1,0:T(8,128)}, f32[4,2,16,512]{3,2,1,0:T(8,128)}) custom-call(f32[2,64,512]{2,1,0:T(8,128)} %bitcast.7, s32[2,64,512]{2,1,0:T(8,128)} %bitcast.8), custom_call_target="tpu_custom_call" | custom-call | flops 1048576 | bytes 1048576 | tf_op jit(solution)/shard_map/pallas_call | solution.py:46
  8.4 35.5 %all_to_all.5.refs_0_ = f32[4,2,16,512]{3,2,1,0:T(8,128)S(1)} all-to-all(f32[4,2,16,512]{3,2,1,0:T(8,128)} %get-tuple-element.12), channel_id=1, replica_groups=mesh['day'=4,'y'=4,'z'=4,'x'=4,'core'=2] {'day'}, dimensions={0} | all-to-all | bytes 524288 | tf_op jit(solution)/shard_map/all_to_all | solution.py:231
  43.9 0.1 shard_map.29
  44.0 17.4 %all_gather.9.refs_1_ = f32[64,512]{1,0:T(8,128)S(1)} all-gather(f32[16,512]{1,0:T(8,128)S(1)} %shard_map.29), channel_id=1, replica_groups=mesh['day'=4,'y'=4,'z'=4,'x'=4,'core'=2] {'day'}, dimensions={0}, use_global_device_ids=true | all-gather | bytes 163840 | tf_op jit(solution)/shard_map/all_gather | solution.py:233
  61.5 0.9 copy-done
  62.4 0.7 shard_map.30
  63.1 6.2 %collective-permute-start = (f32[2,64,512]{2,1,0:T(8,128)}, f32[2,64,512]{2,1,0:T(8,128)S(1)}, u32[]{:S(2)}, u32[]{:S(2)}) collective-permute-start(f32[2,64,512]{2,1,0:T(8,128)} %shard_map.30), channel_id=1, source_target_pairs={{0,0},{1,8},{2,32},{3,40},{4,64},{5,72},{6,96},{7,104},{8,16},{9,2... | collective-permute-start | bytes 786440 | tf_op jit(solution)/shard_map/ppermute | solution.py:236
  69.3 10.0 %collective-permute-done.refs_0_ = f32[2,64,512]{2,1,0:T(8,128)S(1)} collective-permute-done((f32[2,64,512]{2,1,0:T(8,128)}, f32[2,64,512]{2,1,0:T(8,128)S(1)}, u32[]{:S(2)}, u32[]{:S(2)}) %collective-permute-start) | collective-permute-done | bytes 262176 | tf_op jit(solution)/shard_map/ppermute | solution.py:236
  79.3 0.0 all-gather.3.cloned.1.call-update
  79.3 4.0 %collective-permute-start.3 = (f32[2,64,512]{2,1,0:T(8,128)S(1)}, f32[2,64,512]{2,1,0:T(8,128)S(1)}, u32[]{:S(2)}, u32[]{:S(2)}) collective-permute-start(f32[2,64,512]{2,1,0:T(8,128)S(1)} %collective-permute-done.refs_0_), channel_id=1, source_target_pairs={{0,8},{8,16},{16,24},{24,0},{1,9},{9,17},{17,25},{25,1},{2,10},{10... | collective-permute-start | bytes 786440 | tf_op jit(solution)/shard_map/ppermute | solution.py:240
  83.3 5.1 %collective-permute-start.1 = (f32[2,64,512]{2,1,0:T(8,128)S(1)}, f32[2,64,512]{2,1,0:T(8,128)S(1)}, u32[]{:S(2)}, u32[]{:S(2)}) collective-permute-start(f32[2,64,512]{2,1,0:T(8,128)S(1)} %collective-permute-done.refs_0_), channel_id=1, source_target_pairs={{0,16},{8,24},{16,0},{24,8},{1,17},{9,25},{17,1},{25,9},{2,18},{10... | collective-permute-start | bytes 786440 | tf_op jit(solution)/shard_map/ppermute | solution.py:240
  88.4 1.9 %collective-permute-start.2 = (f32[2,64,512]{2,1,0:T(8,128)S(1)}, f32[2,64,512]{2,1,0:T(8,128)S(1)}, u32[]{:S(2)}, u32[]{:S(2)}) collective-permute-start(f32[2,64,512]{2,1,0:T(8,128)S(1)} %collective-permute-done.refs_0_), channel_id=1, source_target_pairs={{0,24},{8,0},{16,8},{24,16},{1,25},{9,1},{17,9},{25,17},{2,26},{10... | collective-permute-start | bytes 786440 | tf_op jit(solution)/shard_map/ppermute | solution.py:240
  90.3 10.2 %collective-permute-done.3.refs_1_ = f32[2,64,512]{2,1,0:T(8,128)S(1)} collective-permute-done((f32[2,64,512]{2,1,0:T(8,128)S(1)}, f32[2,64,512]{2,1,0:T(8,128)S(1)}, u32[]{:S(2)}, u32[]{:S(2)}) %collective-permute-start.3) | collective-permute-done | bytes 262176 | tf_op jit(solution)/shard_map/ppermute | solution.py:240
  100.5 1.9 %collective-permute-start.5 = (f32[4,64,512]{2,1,0:T(8,128)S(1)}, f32[4,64,512]{2,1,0:T(8,128)S(1)}, u32[]{:S(2)}, u32[]{:S(2)}) collective-permute-start(f32[4,64,512]{2,1,0:T(8,128)S(1)} %shard_map.32.b), channel_id=1, source_target_pairs={{0,32},{1,97},{32,64},{33,1},{64,96},{65,33},{96,0},{97,65},{2,34}... | collective-permute-start | bytes 1572872 | tf_op jit(solution)/shard_map/ppermute | solution.py:245
  102.5 1.6 %collective-permute-done.1.refs_0_ = f32[2,64,512]{2,1,0:T(8,128)S(1)} collective-permute-done((f32[2,64,512]{2,1,0:T(8,128)S(1)}, f32[2,64,512]{2,1,0:T(8,128)S(1)}, u32[]{:S(2)}, u32[]{:S(2)}) %collective-permute-start.1) | collective-permute-done | bytes 262176 | tf_op jit(solution)/shard_map/ppermute | solution.py:240
  104.1 3.2 %collective-permute-done.2.refs_1_ = f32[2,64,512]{2,1,0:T(8,128)S(1)} collective-permute-done((f32[2,64,512]{2,1,0:T(8,128)S(1)}, f32[2,64,512]{2,1,0:T(8,128)S(1)}, u32[]{:S(2)}, u32[]{:S(2)}) %collective-permute-start.2) | collective-permute-done | bytes 262176 | tf_op jit(solution)/shard_map/ppermute | solution.py:240
  107.3 1.9 %collective-permute-start.4 = (f32[4,64,512]{2,1,0:T(8,128)S(1)}, f32[4,64,512]{2,1,0:T(8,128)S(1)}, u32[]{:S(2)}, u32[]{:S(2)}) collective-permute-start(f32[4,64,512]{2,1,0:T(8,128)S(1)} %shard_map.31.a), channel_id=1, source_target_pairs={{0,32},{1,97},{32,64},{33,1},{64,96},{65,33},{96,0},{97,65},{2,34}... | collective-permute-start | bytes 1572872 | tf_op jit(solution)/shard_map/ppermute | solution.py:245
  109.2 3.6 %collective-permute-done.5.b_one = f32[4,64,512]{2,1,0:T(8,128)S(1)} collective-permute-done((f32[4,64,512]{2,1,0:T(8,128)S(1)}, f32[4,64,512]{2,1,0:T(8,128)S(1)}, u32[]{:S(2)}, u32[]{:S(2)}) %collective-permute-start.5) | collective-permute-done | bytes 524320 | tf_op jit(solution)/shard_map/ppermute | solution.py:245
  112.8 1.9 %collective-permute-start.7 = (f32[4,64,512]{2,1,0:T(8,128)S(1)}, f32[4,64,512]{2,1,0:T(8,128)}, u32[]{:S(2)}, u32[]{:S(2)}) collective-permute-start(f32[4,64,512]{2,1,0:T(8,128)S(1)} %collective-permute-done.5.b_one), channel_id=1, source_target_pairs={{0,32},{1,97},{32,64},{33,1},{64,96},{65,33},{96,0},{97,65},{2,34}... | collective-permute-start | bytes 1572872 | tf_op jit(solution)/shard_map/ppermute | solution.py:245
  114.7 4.8 %collective-permute-done.4.a_one = f32[4,64,512]{2,1,0:T(8,128)S(1)} collective-permute-done((f32[4,64,512]{2,1,0:T(8,128)S(1)}, f32[4,64,512]{2,1,0:T(8,128)S(1)}, u32[]{:S(2)}, u32[]{:S(2)}) %collective-permute-start.4) | collective-permute-done | bytes 524320 | tf_op jit(solution)/shard_map/ppermute | solution.py:245
  119.6 1.9 %collective-permute-start.6 = (f32[4,64,512]{2,1,0:T(8,128)S(1)}, f32[4,64,512]{2,1,0:T(8,128)}, u32[]{:S(2)}, u32[]{:S(2)}) collective-permute-start(f32[4,64,512]{2,1,0:T(8,128)S(1)} %collective-permute-done.4.a_one), channel_id=1, source_target_pairs={{0,32},{1,97},{32,64},{33,1},{64,96},{65,33},{96,0},{97,65},{2,34}... | collective-permute-start | bytes 1572872 | tf_op jit(solution)/shard_map/ppermute | solution.py:245
  121.5 3.8 %collective-permute-done.7.b_two = f32[4,64,512]{2,1,0:T(8,128)} collective-permute-done((f32[4,64,512]{2,1,0:T(8,128)S(1)}, f32[4,64,512]{2,1,0:T(8,128)}, u32[]{:S(2)}, u32[]{:S(2)}) %collective-permute-start.7) | collective-permute-done | bytes 524320 | tf_op jit(solution)/shard_map/ppermute | solution.py:245
  125.3 1.9 %collective-permute-start.9 = (f32[4,64,512]{2,1,0:T(8,128)}, f32[4,64,512]{2,1,0:T(8,128)S(1)}, u32[]{:S(2)}, u32[]{:S(2)}) collective-permute-start(f32[4,64,512]{2,1,0:T(8,128)} %collective-permute-done.7.b_two), channel_id=1, source_target_pairs={{0,32},{1,97},{32,64},{33,1},{64,96},{65,33},{96,0},{97,65},{2,34}... | collective-permute-start | bytes 1572872 | tf_op jit(solution)/shard_map/ppermute | solution.py:245
  127.2 4.7 %collective-permute-done.6.a_two = f32[4,64,512]{2,1,0:T(8,128)} collective-permute-done((f32[4,64,512]{2,1,0:T(8,128)S(1)}, f32[4,64,512]{2,1,0:T(8,128)}, u32[]{:S(2)}, u32[]{:S(2)}) %collective-permute-start.6) | collective-permute-done | bytes 524320 | tf_op jit(solution)/shard_map/ppermute | solution.py:245
  132.0 1.9 %collective-permute-start.8 = (f32[4,64,512]{2,1,0:T(8,128)}, f32[4,64,512]{2,1,0:T(8,128)S(1)}, u32[]{:S(2)}, u32[]{:S(2)}) collective-permute-start(f32[4,64,512]{2,1,0:T(8,128)} %collective-permute-done.6.a_two), channel_id=1, source_target_pairs={{0,32},{1,97},{32,64},{33,1},{64,96},{65,33},{96,0},{97,65},{2,34}... | collective-permute-start | bytes 1572872 | tf_op jit(solution)/shard_map/ppermute | solution.py:245
  133.9 0.1 pad_add_fusion.where
  134.0 1.6 %copy-done.1 = f32[16,64,512]{2,1,0:T(8,128)S(1)} copy-done((f32[16,64,512]{2,1,0:T(8,128)S(1)}, f32[16,64,512]{2,1,0:T(8,128)}, u32[]{:S(2)}) %copy-start.1) | copy-done | bytes 2097176
  135.6 5.6 %shard_map.33 = (f32[2,512,1024]{2,1,0:T(8,128)}, bf16[2,512,512]{2,1,0:T(8,128)(2,1)S(1)}, bf16[2,512,512]{2,1,0:T(8,128)(2,1)S(1)}) custom-call(s32[3]{0:T(128)S(1)} %pad_add_fusion.where, f32[8,2,64,512]{3,2,1,0:T(8,128)S(1)} %bitcast.6, f32[4,64,512]{2,1,0:T(8,128)S(1)} %shard_map.31.a, f32[4,64,512]{2,1,0:T(8,128)S(1)} %shard_map.32.b, ...), custom_call_target="tpu_custom_call" | custom-call | flops 2415919104 | bytes 3145728 | tf_op jit(solution)/shard_map/pallas_call | solution.py:168
  141.2 0.0 collective-permute-done.9.b
  141.2 3.3 %collective-permute-done.8.a = f32[4,64,512]{2,1,0:T(8,128)S(1)} collective-permute-done((f32[4,64,512]{2,1,0:T(8,128)}, f32[4,64,512]{2,1,0:T(8,128)S(1)}, u32[]{:S(2)}, u32[]{:S(2)}) %collective-permute-start.8) | collective-permute-done | bytes 524320 | tf_op jit(solution)/shard_map/ppermute | solution.py:245
  144.4 2.7 %shard_map.34 = f32[2,512,1024]{2,1,0:T(8,128)} custom-call(s32[3]{0:T(128)S(1)} %pad_add_fusion.where, bf16[2,512,512]{2,1,0:T(8,128)(2,1)S(1)} %get-tuple-element.14.row_high, bf16[2,512,512]{2,1,0:T(8,128)(2,1)S(1)} %get-tuple-element.15.row_low, f32[4,64,512]{2,1,0:T(8,128)S(1)} %collective-permute-done.8.a, ...), custom_call_target="tpu_custom_call", output_to_operand_aliasing={{}: (5, {})} | custom-call | flops 805306368 | bytes 1048576 | tf_op jit(solution)/shard_map/pallas_call | solution.py:190
  (5 shorter events, 0.1 us)
Async XLA Ops:
  6.5 127.4 %all-gather.3.cloned.1.call-start = ((), (), s32[]{:S(2)}) async-start(), calls=%async_computation.1 | async-start | bytes 2359296 | tf_op jit(solution)/shard_map/all_gather | solution.py:238
  61.5 1.0 copy-start
  63.1 16.1 %collective-permute-start = (f32[2,64,512]{2,1,0:T(8,128)}, f32[2,64,512]{2,1,0:T(8,128)S(1)}, u32[]{:S(2)}, u32[]{:S(2)}) collective-permute-start(f32[2,64,512]{2,1,0:T(8,128)} %shard_map.30), channel_id=1, source_target_pairs={{0,0},{1,8},{2,32},{3,40},{4,64},{5,72},{6,96},{7,104},{8,16},{9,2... | collective-permute-start | bytes 786440 | tf_op jit(solution)/shard_map/ppermute | solution.py:236
  79.3 21.2 %collective-permute-start.3 = (f32[2,64,512]{2,1,0:T(8,128)S(1)}, f32[2,64,512]{2,1,0:T(8,128)S(1)}, u32[]{:S(2)}, u32[]{:S(2)}) collective-permute-start(f32[2,64,512]{2,1,0:T(8,128)S(1)} %collective-permute-done.refs_0_), channel_id=1, source_target_pairs={{0,8},{8,16},{16,24},{24,0},{1,9},{9,17},{17,25},{25,1},{2,10},{10... | collective-permute-start | bytes 786440 | tf_op jit(solution)/shard_map/ppermute | solution.py:240
  83.3 20.7 %collective-permute-start.1 = (f32[2,64,512]{2,1,0:T(8,128)S(1)}, f32[2,64,512]{2,1,0:T(8,128)S(1)}, u32[]{:S(2)}, u32[]{:S(2)}) collective-permute-start(f32[2,64,512]{2,1,0:T(8,128)S(1)} %collective-permute-done.refs_0_), channel_id=1, source_target_pairs={{0,16},{8,24},{16,0},{24,8},{1,17},{9,25},{17,1},{25,9},{2,18},{10... | collective-permute-start | bytes 786440 | tf_op jit(solution)/shard_map/ppermute | solution.py:240
  88.4 18.9 %collective-permute-start.2 = (f32[2,64,512]{2,1,0:T(8,128)S(1)}, f32[2,64,512]{2,1,0:T(8,128)S(1)}, u32[]{:S(2)}, u32[]{:S(2)}) collective-permute-start(f32[2,64,512]{2,1,0:T(8,128)S(1)} %collective-permute-done.refs_0_), channel_id=1, source_target_pairs={{0,24},{8,0},{16,8},{24,16},{1,25},{9,1},{17,9},{25,17},{2,26},{10... | collective-permute-start | bytes 786440 | tf_op jit(solution)/shard_map/ppermute | solution.py:240
  100.5 12.3 %collective-permute-start.5 = (f32[4,64,512]{2,1,0:T(8,128)S(1)}, f32[4,64,512]{2,1,0:T(8,128)S(1)}, u32[]{:S(2)}, u32[]{:S(2)}) collective-permute-start(f32[4,64,512]{2,1,0:T(8,128)S(1)} %shard_map.32.b), channel_id=1, source_target_pairs={{0,32},{1,97},{32,64},{33,1},{64,96},{65,33},{96,0},{97,65},{2,34}... | collective-permute-start | bytes 1572872 | tf_op jit(solution)/shard_map/ppermute | solution.py:245
  107.3 12.3 %collective-permute-start.4 = (f32[4,64,512]{2,1,0:T(8,128)S(1)}, f32[4,64,512]{2,1,0:T(8,128)S(1)}, u32[]{:S(2)}, u32[]{:S(2)}) collective-permute-start(f32[4,64,512]{2,1,0:T(8,128)S(1)} %shard_map.31.a), channel_id=1, source_target_pairs={{0,32},{1,97},{32,64},{33,1},{64,96},{65,33},{96,0},{97,65},{2,34}... | collective-permute-start | bytes 1572872 | tf_op jit(solution)/shard_map/ppermute | solution.py:245
  112.8 12.5 %collective-permute-start.7 = (f32[4,64,512]{2,1,0:T(8,128)S(1)}, f32[4,64,512]{2,1,0:T(8,128)}, u32[]{:S(2)}, u32[]{:S(2)}) collective-permute-start(f32[4,64,512]{2,1,0:T(8,128)S(1)} %collective-permute-done.5.b_one), channel_id=1, source_target_pairs={{0,32},{1,97},{32,64},{33,1},{64,96},{65,33},{96,0},{97,65},{2,34}... | collective-permute-start | bytes 1572872 | tf_op jit(solution)/shard_map/ppermute | solution.py:245
  119.6 12.4 %collective-permute-start.6 = (f32[4,64,512]{2,1,0:T(8,128)S(1)}, f32[4,64,512]{2,1,0:T(8,128)}, u32[]{:S(2)}, u32[]{:S(2)}) collective-permute-start(f32[4,64,512]{2,1,0:T(8,128)S(1)} %collective-permute-done.4.a_one), channel_id=1, source_target_pairs={{0,32},{1,97},{32,64},{33,1},{64,96},{65,33},{96,0},{97,65},{2,34}... | collective-permute-start | bytes 1572872 | tf_op jit(solution)/shard_map/ppermute | solution.py:245
  125.3 15.9 %collective-permute-start.9 = (f32[4,64,512]{2,1,0:T(8,128)}, f32[4,64,512]{2,1,0:T(8,128)S(1)}, u32[]{:S(2)}, u32[]{:S(2)}) collective-permute-start(f32[4,64,512]{2,1,0:T(8,128)} %collective-permute-done.7.b_two), channel_id=1, source_target_pairs={{0,32},{1,97},{32,64},{33,1},{64,96},{65,33},{96,0},{97,65},{2,34}... | collective-permute-start | bytes 1572872 | tf_op jit(solution)/shard_map/ppermute | solution.py:245
  132.0 12.5 %collective-permute-start.8 = (f32[4,64,512]{2,1,0:T(8,128)}, f32[4,64,512]{2,1,0:T(8,128)S(1)}, u32[]{:S(2)}, u32[]{:S(2)}) collective-permute-start(f32[4,64,512]{2,1,0:T(8,128)} %collective-permute-done.6.a_two), channel_id=1, source_target_pairs={{0,32},{1,97},{32,64},{33,1},{64,96},{65,33},{96,0},{97,65},{2,34}... | collective-permute-start | bytes 1572872 | tf_op jit(solution)/shard_map/ppermute | solution.py:245
  134.0 1.6 %copy-start.1 = (f32[16,64,512]{2,1,0:T(8,128)S(1)}, f32[16,64,512]{2,1,0:T(8,128)}, u32[]{:S(2)}) copy-start(f32[16,64,512]{2,1,0:T(8,128)} %all-gather.3.cloned.1.call-done) | copy-start | bytes 6291460
Sparse Core Ops, SparseCore 0:
  79.4 27.6 all-gather.2

commit v4 on v2

--- a/solution.py
+++ b/solution.py
@@ -235,7 +235,8 @@
     rows = lax.all_gather(scaled, (X, CORE))
 
     turned = lax.ppermute(scaled, GROUP, turn_pairs())
-    z1, z2, z3 = [lax.ppermute(turned, Z, shift(step)) for step in (1, 2, 3)]
+    z1, z3 = [lax.ppermute(turned, Z, shift(step)) for step in (1, 3)]
+    z2 = lax.ppermute(z1, Z, shift(1))
     (b,) = local(pair_kernel, [shape(4, size, bins)], turned, z1)
     (a,) = local(pair_kernel, [shape(4, size, bins)], z2, z3)
     units = [a, b]

time: 154 us -> 151 us (0.981)
  the two profiles are of different devices: /device:TPU:36 before, /device:TPU:4 now
where the time goes in v4:
time: 151 us; the launch traced here: 150 us
  blocking collectives  51.4 us (34%)
  waiting for transfers between devices  46.5 us (31%)
  starting transfers between devices  26.1 us (17%)
  between operations  13.5 us (9%)
  Pallas kernels  9.31 us (6%)
  local copies, waits for them, and re-layouts  3.49 us (2%)
    all_to_all x1, blocking collectives, body(): sums = lax.all_to_all(sums, DAY, 0, 0)  33.6 us
    ppermute x6, waiting for transfers between devices, body(): lax.ppermute(unit, (Y, CORE), ring_pairs())  20.2 us
    all_gather x1, blocking collectives, body(): weight = lax.all_gather(weight, DAY, axis=0, tiled=True)  17.8 us
    ppermute x1, waiting for transfers between devices, body(): turned = lax.ppermute(scaled, GROUP, turn_pairs())  15.2 us
    ppermute x6, starting transfers between devices, body(): lax.ppermute(unit, (Y, CORE), ring_pairs())  11.5 us
    ppermute x2, starting transfers between devices, body(): z1, z3 = [lax.ppermute(turned, Z, shift(step)) for step in (1, 3)]  7.63 us
    ppermute x2, waiting for transfers between devices, body(): z1, z3 = [lax.ppermute(turned, Z, shift(step)) for step in (1, 3)]  5.91 us
    pallas_call x1, Pallas kernels, near_product(): pl.pallas_call(near_kernel, in_specs=[SCALARS] + [WHOLE] * (1 + len(block...  5.6 us
  transfers between devices with their start and end apart: 11, of which 9 were waited for; matrix products, arithmetic and copies ran while one was open for 0% of the time, Pallas kernels for 4%

profile of v4, /device:TPU:4, one launch (start us, length us, event | category | flops | bytes accessed | tf_op | source)
XLA Modules:
  0.0 150.4 jit_solution(12602068016502021070)
XLA Ops:
  6.5 0.9 copy-done
  7.5 0.9 copy-done.1
  8.4 0.1 shard_map.28
  8.5 33.6 %all_to_all.5.refs_0_ = f32[4,2,16,512]{3,2,1,0:T(8,128)S(1)} all-to-all(f32[4,2,16,512]{3,2,1,0:T(8,128)S(1)} %get-tuple-element.11), channel_id=1, replica_groups=mesh['day'=4,'y'=4,'z'=4,'x'=4,'core'=2] {'day'}, dimensions={0} | all-to-all | bytes 524288 | tf_op jit(solution)/shard_map/all_to_all | solution.py:230
  42.2 0.1 shard_map.29
  42.3 17.8 %all_gather.9.refs_1_ = f32[64,512]{1,0:T(8,128)S(1)} all-gather(f32[16,512]{1,0:T(8,128)S(1)} %shard_map.29), channel_id=1, replica_groups=mesh['day'=4,'y'=4,'z'=4,'x'=4,'core'=2] {'day'}, dimensions={0}, use_global_device_ids=true | all-gather | bytes 163840 | tf_op jit(solution)/shard_map/all_gather | solution.py:232
  60.1 0.7 shard_map.30
  60.8 0.0 all-gather.3.cloned.1.call-update
  60.8 5.0 %collective-permute-start = (f32[2,64,512]{2,1,0:T(8,128)}, f32[2,64,512]{2,1,0:T(8,128)S(1)}, u32[]{:S(2)}, u32[]{:S(2)}) collective-permute-start(f32[2,64,512]{2,1,0:T(8,128)} %shard_map.30), channel_id=1, source_target_pairs={{0,0},{1,8},{2,32},{3,40},{4,64},{5,72},{6,96},{7,104},{8,16},{9,2... | collective-permute-start | bytes 786440 | tf_op jit(solution)/shard_map/ppermute | solution.py:237
  65.9 15.2 %collective-permute-done.refs_0_ = f32[2,64,512]{2,1,0:T(8,128)S(1)} collective-permute-done((f32[2,64,512]{2,1,0:T(8,128)}, f32[2,64,512]{2,1,0:T(8,128)S(1)}, u32[]{:S(2)}, u32[]{:S(2)}) %collective-permute-start) | collective-permute-done | bytes 262176 | tf_op jit(solution)/shard_map/ppermute | solution.py:237
  81.1 1.9 %collective-permute-start.1 = (f32[2,64,512]{2,1,0:T(8,128)S(1)}, f32[2,64,512]{2,1,0:T(8,128)S(1)}, u32[]{:S(2)}, u32[]{:S(2)}) collective-permute-start(f32[2,64,512]{2,1,0:T(8,128)S(1)} %collective-permute-done.refs_0_), channel_id=1, source_target_pairs={{0,8},{8,16},{16,24},{24,0},{1,9},{9,17},{17,25},{25,1},{2,10},{10... | collective-permute-start | bytes 786440 | tf_op jit(solution)/shard_map/ppermute | solution.py:238
  83.0 5.7 %collective-permute-start.3 = (f32[2,64,512]{2,1,0:T(8,128)S(1)}, f32[2,64,512]{2,1,0:T(8,128)S(1)}, u32[]{:S(2)}, u32[]{:S(2)}) collective-permute-start(f32[2,64,512]{2,1,0:T(8,128)S(1)} %collective-permute-done.refs_0_), channel_id=1, source_target_pairs={{0,24},{8,0},{16,8},{24,16},{1,25},{9,1},{17,9},{25,17},{2,26},{10... | collective-permute-start | bytes 786440 | tf_op jit(solution)/shard_map/ppermute | solution.py:238
  88.7 4.9 %collective-permute-done.1.refs_1_ = f32[2,64,512]{2,1,0:T(8,128)S(1)} collective-permute-done((f32[2,64,512]{2,1,0:T(8,128)S(1)}, f32[2,64,512]{2,1,0:T(8,128)S(1)}, u32[]{:S(2)}, u32[]{:S(2)}) %collective-permute-start.1) | collective-permute-done | bytes 262176 | tf_op jit(solution)/shard_map/ppermute | solution.py:238
  93.6 1.9 %collective-permute-start.2 = (f32[2,64,512]{2,1,0:T(8,128)S(1)}, f32[2,64,512]{2,1,0:T(8,128)S(1)}, u32[]{:S(2)}, u32[]{:S(2)}) collective-permute-start(f32[2,64,512]{2,1,0:T(8,128)S(1)} %collective-permute-done.1.refs_1_), channel_id=1, source_target_pairs={{0,8},{8,16},{16,24},{24,0},{1,9},{9,17},{17,25},{25,1},{2,10},{10... | collective-permute-start | bytes 786440 | tf_op jit(solution)/shard_map/ppermute | solution.py:239
  95.6 1.9 %collective-permute-start.5 = (f32[4,64,512]{2,1,0:T(8,128)S(1)}, f32[4,64,512]{2,1,0:T(8,128)S(1)}, u32[]{:S(2)}, u32[]{:S(2)}) collective-permute-start(f32[4,64,512]{2,1,0:T(8,128)S(1)} %shard_map.32.b), channel_id=1, source_target_pairs={{0,32},{1,97},{32,64},{33,1},{64,96},{65,33},{96,0},{97,65},{2,34}... | collective-permute-start | bytes 1572872 | tf_op jit(solution)/shard_map/ppermute | solution.py:244
  97.5 1.0 collective-permute-done.3.refs_1_
  98.5 5.1 %collective-permute-done.2.refs_0_ = f32[2,64,512]{2,1,0:T(8,128)S(1)} collective-permute-done((f32[2,64,512]{2,1,0:T(8,128)S(1)}, f32[2,64,512]{2,1,0:T(8,128)S(1)}, u32[]{:S(2)}, u32[]{:S(2)}) %collective-permute-start.2) | collective-permute-done | bytes 262176 | tf_op jit(solution)/shard_map/ppermute | solution.py:239
  103.7 1.9 %collective-permute-start.4 = (f32[4,64,512]{2,1,0:T(8,128)S(1)}, f32[4,64,512]{2,1,0:T(8,128)S(1)}, u32[]{:S(2)}, u32[]{:S(2)}) collective-permute-start(f32[4,64,512]{2,1,0:T(8,128)S(1)} %shard_map.31.a), channel_id=1, source_target_pairs={{0,32},{1,97},{32,64},{33,1},{64,96},{65,33},{96,0},{97,65},{2,34}... | collective-permute-start | bytes 1572872 | tf_op jit(solution)/shard_map/ppermute | solution.py:244
  105.6 2.2 %collective-permute-done.5.b_one = f32[4,64,512]{2,1,0:T(8,128)S(1)} collective-permute-done((f32[4,64,512]{2,1,0:T(8,128)S(1)}, f32[4,64,512]{2,1,0:T(8,128)S(1)}, u32[]{:S(2)}, u32[]{:S(2)}) %collective-permute-start.5) | collective-permute-done | bytes 524320 | tf_op jit(solution)/shard_map/ppermute | solution.py:244
  107.9 1.9 %collective-permute-start.7 = (f32[4,64,512]{2,1,0:T(8,128)S(1)}, f32[4,64,512]{2,1,0:T(8,128)}, u32[]{:S(2)}, u32[]{:S(2)}) collective-permute-start(f32[4,64,512]{2,1,0:T(8,128)S(1)} %collective-permute-done.5.b_one), channel_id=1, source_target_pairs={{0,32},{1,97},{32,64},{33,1},{64,96},{65,33},{96,0},{97,65},{2,34}... | collective-permute-start | bytes 1572872 | tf_op jit(solution)/shard_map/ppermute | solution.py:244
  109.8 6.2 %collective-permute-done.4.a_one = f32[4,64,512]{2,1,0:T(8,128)S(1)} collective-permute-done((f32[4,64,512]{2,1,0:T(8,128)S(1)}, f32[4,64,512]{2,1,0:T(8,128)S(1)}, u32[]{:S(2)}, u32[]{:S(2)}) %collective-permute-start.4) | collective-permute-done | bytes 524320 | tf_op jit(solution)/shard_map/ppermute | solution.py:244
  116.0 1.9 %collective-permute-start.6 = (f32[4,64,512]{2,1,0:T(8,128)S(1)}, f32[4,64,512]{2,1,0:T(8,128)}, u32[]{:S(2)}, u32[]{:S(2)}) collective-permute-start(f32[4,64,512]{2,1,0:T(8,128)S(1)} %collective-permute-done.4.a_one), channel_id=1, source_target_pairs={{0,32},{1,97},{32,64},{33,1},{64,96},{65,33},{96,0},{97,65},{2,34}... | collective-permute-start | bytes 1572872 | tf_op jit(solution)/shard_map/ppermute | solution.py:244
  117.9 3.8 %collective-permute-done.7.b_two = f32[4,64,512]{2,1,0:T(8,128)} collective-permute-done((f32[4,64,512]{2,1,0:T(8,128)S(1)}, f32[4,64,512]{2,1,0:T(8,128)}, u32[]{:S(2)}, u32[]{:S(2)}) %collective-permute-start.7) | collective-permute-done | bytes 524320 | tf_op jit(solution)/shard_map/ppermute | solution.py:244
  121.7 1.9 %collective-permute-start.9 = (f32[4,64,512]{2,1,0:T(8,128)}, f32[4,64,512]{2,1,0:T(8,128)S(1)}, u32[]{:S(2)}, u32[]{:S(2)}) collective-permute-start(f32[4,64,512]{2,1,0:T(8,128)} %collective-permute-done.7.b_two), channel_id=1, source_target_pairs={{0,32},{1,97},{32,64},{33,1},{64,96},{65,33},{96,0},{97,65},{2,34}... | collective-permute-start | bytes 1572872 | tf_op jit(solution)/shard_map/ppermute | solution.py:244
  123.6 4.7 %collective-permute-done.6.a_two = f32[4,64,512]{2,1,0:T(8,128)} collective-permute-done((f32[4,64,512]{2,1,0:T(8,128)S(1)}, f32[4,64,512]{2,1,0:T(8,128)}, u32[]{:S(2)}, u32[]{:S(2)}) %collective-permute-start.6) | collective-permute-done | bytes 524320 | tf_op jit(solution)/shard_map/ppermute | solution.py:244
  128.4 1.9 %collective-permute-start.8 = (f32[4,64,512]{2,1,0:T(8,128)}, f32[4,64,512]{2,1,0:T(8,128)S(1)}, u32[]{:S(2)}, u32[]{:S(2)}) collective-permute-start(f32[4,64,512]{2,1,0:T(8,128)} %collective-permute-done.6.a_two), channel_id=1, source_target_pairs={{0,32},{1,97},{32,64},{33,1},{64,96},{65,33},{96,0},{97,65},{2,34}... | collective-permute-start | bytes 1572872 | tf_op jit(solution)/shard_map/ppermute | solution.py:244
  130.3 0.1 pad_add_fusion.where
  130.4 1.6 %copy-done.2 = f32[16,64,512]{2,1,0:T(8,128)S(1)} copy-done((f32[16,64,512]{2,1,0:T(8,128)S(1)}, f32[16,64,512]{2,1,0:T(8,128)}, u32[]{:S(2)}) %copy-start.2) | copy-done | bytes 2097176
  132.0 5.6 %shard_map.33 = (f32[2,512,1024]{2,1,0:T(8,128)}, bf16[2,512,512]{2,1,0:T(8,128)(2,1)S(1)}, bf16[2,512,512]{2,1,0:T(8,128)(2,1)S(1)}) custom-call(s32[3]{0:T(128)S(1)} %pad_add_fusion.where, f32[8,2,64,512]{3,2,1,0:T(8,128)S(1)} %bitcast.8, f32[4,64,512]{2,1,0:T(8,128)S(1)} %shard_map.31.a, f32[4,64,512]{2,1,0:T(8,128)S(1)} %shard_map.32.b, ...), custom_call_target="tpu_custom_call" | custom-call | flops 2415919104 | bytes 3145728 | tf_op jit(solution)/shard_map/pallas_call | solution.py:168
  137.6 0.0 collective-permute-done.9.b
  137.6 3.3 %collective-permute-done.8.a = f32[4,64,512]{2,1,0:T(8,128)S(1)} collective-permute-done((f32[4,64,512]{2,1,0:T(8,128)}, f32[4,64,512]{2,1,0:T(8,128)S(1)}, u32[]{:S(2)}, u32[]{:S(2)}) %collective-permute-start.8) | collective-permute-done | bytes 524320 | tf_op jit(solution)/shard_map/ppermute | solution.py:244
  140.8 2.7 %shard_map.34 = f32[2,512,1024]{2,1,0:T(8,128)} custom-call(s32[3]{0:T(128)S(1)} %pad_add_fusion.where, bf16[2,512,512]{2,1,0:T(8,128)(2,1)S(1)} %get-tuple-element.12.row_high, bf16[2,512,512]{2,1,0:T(8,128)(2,1)S(1)} %get-tuple-element.13.row_low, f32[4,64,512]{2,1,0:T(8,128)S(1)} %collective-permute-done.8.a, ...), custom_call_target="tpu_custom_call", output_to_operand_aliasing={{}: (5, {})} | custom-call | flops 805306368 | bytes 1048576 | tf_op jit(solution)/shard_map/pallas_call | solution.py:190
  (7 shorter events, 0.1 us)
Async XLA Ops:
  6.5 123.8 %all-gather.3.cloned.1.call-start = ((), (), s32[]{:S(2)}) async-start(), calls=%async_computation.1 | async-start | bytes 2359296 | tf_op jit(solution)/shard_map/all_gather | solution.py:235
  6.5 0.9 copy-start
  7.5 0.9 copy-start.1
  60.8 20.3 %collective-permute-start = (f32[2,64,512]{2,1,0:T(8,128)}, f32[2,64,512]{2,1,0:T(8,128)S(1)}, u32[]{:S(2)}, u32[]{:S(2)}) collective-permute-start(f32[2,64,512]{2,1,0:T(8,128)} %shard_map.30), channel_id=1, source_target_pairs={{0,0},{1,8},{2,32},{3,40},{4,64},{5,72},{6,96},{7,104},{8,16},{9,2... | collective-permute-start | bytes 786440 | tf_op jit(solution)/shard_map/ppermute | solution.py:237
  81.1 12.5 %collective-permute-start.1 = (f32[2,64,512]{2,1,0:T(8,128)S(1)}, f32[2,64,512]{2,1,0:T(8,128)S(1)}, u32[]{:S(2)}, u32[]{:S(2)}) collective-permute-start(f32[2,64,512]{2,1,0:T(8,128)S(1)} %collective-permute-done.refs_0_), channel_id=1, source_target_pairs={{0,8},{8,16},{16,24},{24,0},{1,9},{9,17},{17,25},{25,1},{2,10},{10... | collective-permute-start | bytes 786440 | tf_op jit(solution)/shard_map/ppermute | solution.py:238
  83.0 15.5 %collective-permute-start.3 = (f32[2,64,512]{2,1,0:T(8,128)S(1)}, f32[2,64,512]{2,1,0:T(8,128)S(1)}, u32[]{:S(2)}, u32[]{:S(2)}) collective-permute-start(f32[2,64,512]{2,1,0:T(8,128)S(1)} %collective-permute-done.refs_0_), channel_id=1, source_target_pairs={{0,24},{8,0},{16,8},{24,16},{1,25},{9,1},{17,9},{25,17},{2,26},{10... | collective-permute-start | bytes 786440 | tf_op jit(solution)/shard_map/ppermute | solution.py:238
  93.6 10.1 %collective-permute-start.2 = (f32[2,64,512]{2,1,0:T(8,128)S(1)}, f32[2,64,512]{2,1,0:T(8,128)S(1)}, u32[]{:S(2)}, u32[]{:S(2)}) collective-permute-start(f32[2,64,512]{2,1,0:T(8,128)S(1)} %collective-permute-done.1.refs_1_), channel_id=1, source_target_pairs={{0,8},{8,16},{16,24},{24,0},{1,9},{9,17},{17,25},{25,1},{2,10},{10... | collective-permute-start | bytes 786440 | tf_op jit(solution)/shard_map/ppermute | solution.py:239
  95.6 12.3 %collective-permute-start.5 = (f32[4,64,512]{2,1,0:T(8,128)S(1)}, f32[4,64,512]{2,1,0:T(8,128)S(1)}, u32[]{:S(2)}, u32[]{:S(2)}) collective-permute-start(f32[4,64,512]{2,1,0:T(8,128)S(1)} %shard_map.32.b), channel_id=1, source_target_pairs={{0,32},{1,97},{32,64},{33,1},{64,96},{65,33},{96,0},{97,65},{2,34}... | collective-permute-start | bytes 1572872 | tf_op jit(solution)/shard_map/ppermute | solution.py:244
  103.7 12.3 %collective-permute-start.4 = (f32[4,64,512]{2,1,0:T(8,128)S(1)}, f32[4,64,512]{2,1,0:T(8,128)S(1)}, u32[]{:S(2)}, u32[]{:S(2)}) collective-permute-start(f32[4,64,512]{2,1,0:T(8,128)S(1)} %shard_map.31.a), channel_id=1, source_target_pairs={{0,32},{1,97},{32,64},{33,1},{64,96},{65,33},{96,0},{97,65},{2,34}... | collective-permute-start | bytes 1572872 | tf_op jit(solution)/shard_map/ppermute | solution.py:244
  107.9 13.9 %collective-permute-start.7 = (f32[4,64,512]{2,1,0:T(8,128)S(1)}, f32[4,64,512]{2,1,0:T(8,128)}, u32[]{:S(2)}, u32[]{:S(2)}) collective-permute-start(f32[4,64,512]{2,1,0:T(8,128)S(1)} %collective-permute-done.5.b_one), channel_id=1, source_target_pairs={{0,32},{1,97},{32,64},{33,1},{64,96},{65,33},{96,0},{97,65},{2,34}... | collective-permute-start | bytes 1572872 | tf_op jit(solution)/shard_map/ppermute | solution.py:244
  116.0 12.4 %collective-permute-start.6 = (f32[4,64,512]{2,1,0:T(8,128)S(1)}, f32[4,64,512]{2,1,0:T(8,128)}, u32[]{:S(2)}, u32[]{:S(2)}) collective-permute-start(f32[4,64,512]{2,1,0:T(8,128)S(1)} %collective-permute-done.4.a_one), channel_id=1, source_target_pairs={{0,32},{1,97},{32,64},{33,1},{64,96},{65,33},{96,0},{97,65},{2,34}... | collective-permute-start | bytes 1572872 | tf_op jit(solution)/shard_map/ppermute | solution.py:244
  121.7 15.9 %collective-permute-start.9 = (f32[4,64,512]{2,1,0:T(8,128)}, f32[4,64,512]{2,1,0:T(8,128)S(1)}, u32[]{:S(2)}, u32[]{:S(2)}) collective-permute-start(f32[4,64,512]{2,1,0:T(8,128)} %collective-permute-done.7.b_two), channel_id=1, source_target_pairs={{0,32},{1,97},{32,64},{33,1},{64,96},{65,33},{96,0},{97,65},{2,34}... | collective-permute-start | bytes 1572872 | tf_op jit(solution)/shard_map/ppermute | solution.py:244
  128.4 12.5 %collective-permute-start.8 = (f32[4,64,512]{2,1,0:T(8,128)}, f32[4,64,512]{2,1,0:T(8,128)S(1)}, u32[]{:S(2)}, u32[]{:S(2)}) collective-permute-start(f32[4,64,512]{2,1,0:T(8,128)} %collective-permute-done.6.a_two), channel_id=1, source_target_pairs={{0,32},{1,97},{32,64},{33,1},{64,96},{65,33},{96,0},{97,65},{2,34}... | collective-permute-start | bytes 1572872 | tf_op jit(solution)/shard_map/ppermute | solution.py:244
  130.4 1.6 %copy-start.2 = (f32[16,64,512]{2,1,0:T(8,128)S(1)}, f32[16,64,512]{2,1,0:T(8,128)}, u32[]{:S(2)}) copy-start(f32[16,64,512]{2,1,0:T(8,128)} %all-gather.3.cloned.1.call-done) | copy-start | bytes 6291460
Sparse Core Ops, SparseCore 0:
  61.0 31.2 all-gather.2
